TPU v7x, 512 devices: a whole 4x8x8 slice. The times are simulated.
512 devices in a mesh: traj: 32 (over x, y), cand: 16 (over z, core).
Axes of the slice: x: 4, y: 8, z: 8, core: 2. Of those that a mesh axis runs over, the one named last changes fastest.
Arguments:
- state: float32 [4096, 256], P('traj'), may hold values from -6 to 6
- target: float32 [4096, 256], P('traj'), may hold values from -6 to 6
- coeffs: bfloat16 [33280, 256], P('cand'), may hold values from -6 to 6
- pairs: int32 [2, 33280], P(None, 'cand'), may hold values from 0 to 256, as said below
- mask: int32 [33280, 256], P('cand'), may hold values 0 or 1
Outputs:
- slope: float32 [4096, 256], P('traj')
- new_coeffs: bfloat16 [33280, 256], P('cand')
Inputs may be any that keep to these rules, and one draw needn't show every extreme that they name: Each column holds a pair pairs[0, c] <= pairs[1, c]; index 256 stands for the constant 1; no pair repeats before every pair has appeared.
All inputs are finite; a program needn't handle non-finite values. No bound on the sum of `mask` on one device may be relied on, other than what follows from the above.
Results may differ from a plain program's by a relative error of at most 0.014.
Values may be sent and summed in bfloat16 or wider, within the bound.
No kernel may reach another device: no remote copies, remote signals or barrier semaphores. Data moves between devices by JAX's collectives and lax.ppermute only.
A program may use at most 64 MiB of HBM per device.

v0:
```python
import math

import jax
import jax.numpy as jnp
from jax import lax
from jax.sharding import PartitionSpec as P

CANDS = 33280


step_dt = 0.25


def body(state, target, coeffs, pairs, mask):
    rows, modes_count = state.shape
    left = pairs[0]
    right = pairs[1]
    scale = 1.0 / math.sqrt(CANDS)
    segments = rows * lax.axis_size("traj")
    modes = jnp.arange(modes_count, dtype=jnp.int32)
    jac_left = (left[:, None] == modes[None, :]).astype(jnp.bfloat16)
    jac_right = (right[:, None] == modes[None, :]).astype(jnp.bfloat16)
    ones_col = jnp.ones((rows, 1), jnp.float32)

    def factors(y):
        z = jnp.concatenate([y, ones_col], 1)
        return (jnp.take(z, left, axis=1), jnp.take(z, right, axis=1))

    def library(y):
        left_vals, right_vals = factors(y)
        return (left_vals * right_vals).astype(jnp.bfloat16)

    def derive(theta):
        partial_rate = jnp.dot(theta, coeffs, preferred_element_type=jnp.float32) * scale
        return lax.psum(partial_rate, "cand")

    def pullback(cot, y):
        hidden = (
            lax.dot_general(
                cot.astype(jnp.bfloat16),
                coeffs,
                (((1,), (1,)), ((), ())),
                preferred_element_type=jnp.float32,
            )
            * scale
        )
        left_vals, right_vals = factors(y)
        upper = (hidden * right_vals).astype(jnp.bfloat16)
        lower = (hidden * left_vals).astype(jnp.bfloat16)
        partial_cot = jnp.dot(upper, jac_left, preferred_element_type=jnp.float32)
        partial_cot = partial_cot + jnp.dot(lower, jac_right, preferred_element_type=jnp.float32)
        return lax.psum(partial_cot, "cand")

    y_two = None
    th1 = library(state)
    k1 = derive(th1)
    y_two = state + 0.5 * step_dt * k1
    th2 = library(y_two)
    k2 = derive(th2)
    y_three = state + 0.5 * step_dt * k2
    th3 = library(y_three)
    k3 = derive(th3)
    y_four = state + step_dt * k3
    th4 = library(y_four)
    k4 = derive(th4)
    slope = (k1 + 2.0 * k2 + 2.0 * k3 + k4) / 6.0
    cot = (state + step_dt * slope - target) / segments
    g4 = step_dt / 6.0 * cot
    c4 = pullback(g4, y_four)
    g3 = step_dt / 3.0 * cot + step_dt * c4
    c3 = pullback(g3, y_three)
    g2 = step_dt / 3.0 * cot + 0.5 * step_dt * c3
    c2 = pullback(g2, y_two)
    g1 = step_dt / 6.0 * cot + 0.5 * step_dt * c2

    def outer(theta, grad_cot):
        return lax.dot_general(
            theta,
            grad_cot.astype(jnp.bfloat16),
            (((0,), (0,)), ((), ())),
            preferred_element_type=jnp.float32,
        )

    grad = (outer(th1, g1) + outer(th2, g2) + outer(th3, g3) + outer(th4, g4)) * scale
    rate = 0.5 * math.sqrt(segments * CANDS) / step_dt
    total = lax.psum(grad, "traj")
    fresh = (mask.astype(jnp.float32) * (coeffs.astype(jnp.float32) - rate * total)).astype(
        jnp.bfloat16
    )
    return (slope, fresh)


def solution(mesh):
    placed = (P("traj", None), P("traj", None), P("cand", None), P(None, "cand"), P("cand", None))
    return jax.shard_map(
        body,
        mesh=mesh,
        in_specs=placed,
        out_specs=(P("traj", None), P("cand", None)),
        check_vma=False,
    )
```

profile of v0, /device:TPU:8, one launch (start us, length us, event | category | flops | bytes accessed | tf_op | source)
XLA Modules:
  0.0 1063.9 jit_solution(13873290852304407379)
XLA Ops:
  7.2 0.8 slice_reduce_fusion.1
  8.1 1.0 copy.7
  9.1 3.9 gather_fusion.1
  13.1 5.1 gather_fusion
  18.2 3.0 fusion.19
  21.2 1.0 convolution_multiply_fusion.6
  22.2 0.0 all-reduce.15.cloned.1.call-start
  22.2 118.3 %all-reduce.13.cloned.1.call-done = f32[128,256]{1,0:T(8,128)} async-done(((f32[128,256]{1,0:T(8,128)}), f32[128,256]{1,0:T(8,128)}) %all-reduce.13.cloned.1.call-update) | async-done | bytes 131088 | tf_op jit(solution)/shard_map/psum | solution.py:35
  140.5 0.9 multiply_add_fusion.2
  141.4 0.1 copy.14
  141.6 3.9 gather_fusion.3
  145.5 3.9 gather_fusion.2
  149.5 1.4 fusion.16
  150.9 0.8 copy-done.5
  151.7 1.0 convolution_multiply_fusion.5
  152.7 0.0 all-reduce.17.cloned.1.call-start
  152.8 113.5 %all-reduce.15.cloned.1.call-done = f32[128,256]{1,0:T(8,128)} async-done(((f32[128,256]{1,0:T(8,128)}), f32[128,256]{1,0:T(8,128)}) %all-reduce.15.cloned.1.call-update) | async-done | bytes 131088 | tf_op jit(solution)/shard_map/psum | solution.py:35
  266.3 0.9 multiply_add_fusion.1
  267.2 0.8 copy.15
  268.0 0.9 concatenate.17.clone
  268.9 5.1 gather_fusion.5
  274.0 5.0 gather_fusion.4
  279.0 3.1 fusion.13
  282.1 0.8 copy-done.6
  282.9 1.0 convolution_multiply_fusion.4
  283.9 0.0 all-reduce.19.cloned.1.call-start
  284.0 113.5 %all-reduce.17.cloned.1.call-done = f32[128,256]{1,0:T(8,128)} async-done(((f32[128,256]{1,0:T(8,128)}), f32[128,256]{1,0:T(8,128)}) %all-reduce.17.cloned.1.call-update) | async-done | bytes 131088 | tf_op jit(solution)/shard_map/psum | solution.py:35
  397.5 0.9 multiply_add_fusion
  398.4 0.8 copy.16
  399.2 0.9 concatenate.18.clone
  400.1 5.1 gather_fusion.7
  405.2 5.0 gather_fusion.6
  410.2 3.1 fusion.10
  413.3 0.8 copy-done.8
  414.1 1.0 convolution_multiply_fusion.3
  415.2 113.5 %all-reduce.19.cloned.1.call-done = f32[128,256]{1,0:T(8,128)} async-done(((f32[128,256]{1,0:T(8,128)}), f32[128,256]{1,0:T(8,128)}) %all-reduce.19.cloned.1.call-update) | async-done | bytes 131088 | tf_op jit(solution)/shard_map/psum | solution.py:35
  528.7 1.9 add_subtract_fusion
  530.6 0.4 convolution_multiply_fusion.2
  531.0 0.8 copy-done.4
  531.8 1.0 fusion.3
  532.8 0.2 copy-done.3
  533.0 1.7 fusion.7
  534.8 113.5 %all-reduce.21.cloned.1.call-done = f32[128,256]{1,0:T(8,128)} async-done(((f32[128,256]{1,0:T(8,128)}), f32[128,256]{1,0:T(8,128)}) %all-reduce.21.cloned.1.call-update) | async-done | bytes 131088 | tf_op jit(solution)/shard_map/psum | solution.py:52
  648.3 0.9 add_convert_fusion.2
  649.2 0.4 convolution_multiply_fusion.1
  649.7 0.8 copy-done.2
  650.5 1.0 fusion.2
  651.5 0.2 copy-done.1
  651.7 1.7 fusion.8
  653.4 0.2 all-reduce.25.cloned.1.call-start
  653.6 113.3 %all-reduce.23.cloned.1.call-done = f32[128,256]{1,0:T(8,128)} async-done(((f32[128,256]{1,0:T(8,128)}), f32[128,256]{1,0:T(8,128)}) %all-reduce.23.cloned.1.call-update) | async-done | bytes 131088 | tf_op jit(solution)/shard_map/psum | solution.py:52
  766.9 0.9 add_convert_fusion.1
  767.9 0.4 convolution_multiply_fusion
  768.3 1.0 fusion.1
  769.3 1.7 fusion.9
  771.1 113.5 %all-reduce.25.cloned.1.call-done = f32[128,256]{1,0:T(8,128)} async-done(((f32[128,256]{1,0:T(8,128)}), f32[128,256]{1,0:T(8,128)}) %all-reduce.25.cloned.1.call-update) | async-done | bytes 131088 | tf_op jit(solution)/shard_map/psum | solution.py:52
  884.6 1.3 fusion.44
  885.9 1.5 convolution_add_fusion.2
  887.4 0.4 convolution_add_fusion.1
  887.9 0.6 copy-done.9
  888.5 1.8 fusion
  890.3 0.7 broadcast_multiply_fusion
  891.0 163.1 %all-reduce.27.cloned.1.call-done = f32[2080,256]{1,0:T(8,128)} async-done(((f32[2080,256]{1,0:T(8,128)}), f32[2080,256]{1,0:T(8,128)}) %all-reduce.27.cloned.1.call-update) | async-done | bytes 2129936 | tf_op jit(solution)/shard_map/psum | solution.py:86
  1054.1 3.0 multiply_convert_fusion
  (40 shorter events, 0.4 us)
Async XLA Ops:
  7.2 133.3 %all-reduce.13.cloned.1.call-start = ((), (), s32[]{:S(2)}) async-start(), calls=%async_computation | async-start | bytes 262144 | tf_op jit(solution)/shard_map/psum | solution.py:35
  18.1 3.0 copy-start
  21.1 120.3 %copy-start.10 = (bf16[128,2080]{0,1:T(8,128)(2,1)}, bf16[128,2080]{0,1:T(8,128)(2,1)S(1)}, u32[]{:S(2)}) copy-start(bf16[128,2080]{0,1:T(8,128)(2,1)S(1)} %fusion.19) | copy-start | bytes 1597444
  21.1 119.4 %copy-start.12 = (f32[128,256]{1,0:T(8,128)S(1)}, f32[128,256]{1,0:T(8,128)}, u32[]{:S(2)}) copy-start(f32[128,256]{1,0:T(8,128)} %param.7) | copy-start | bytes 393220
  22.2 244.1 %all-reduce.15.cloned.1.call-start = ((), (), s32[]{:S(2)}) async-start(), calls=%async_computation.1 | async-start | bytes 262144 | tf_op jit(solution)/shard_map/psum | solution.py:35
  150.9 0.8 copy-start.5
  152.7 244.8 %all-reduce.17.cloned.1.call-start = ((), (), s32[]{:S(2)}) async-start(), calls=%async_computation.2 | async-start | bytes 262144 | tf_op jit(solution)/shard_map/psum | solution.py:35
  282.1 0.8 copy-start.6
  283.9 244.8 %all-reduce.19.cloned.1.call-start = ((), (), s32[]{:S(2)}) async-start(), calls=%async_computation.3 | async-start | bytes 262144 | tf_op jit(solution)/shard_map/psum | solution.py:35
  413.3 0.8 copy-start.8
  415.1 233.2 %all-reduce.21.cloned.1.call-start = ((), (), s32[]{:S(2)}) async-start(), calls=%async_computation.4 | async-start | bytes 262144 | tf_op jit(solution)/shard_map/psum | solution.py:52
  530.6 1.2 copy-start.4
  531.8 1.2 copy-start.3
  534.7 232.2 %all-reduce.23.cloned.1.call-start = ((), (), s32[]{:S(2)}) async-start(), calls=%async_computation.5 | async-start | bytes 262144 | tf_op jit(solution)/shard_map/psum | solution.py:52
  649.2 1.2 copy-start.2
  650.5 1.2 copy-start.1
  653.4 231.2 %all-reduce.25.cloned.1.call-start = ((), (), s32[]{:S(2)}) async-start(), calls=%async_computation.6 | async-start | bytes 262144 | tf_op jit(solution)/shard_map/psum | solution.py:52
  769.3 115.3 %copy-start.11 = (bf16[128,2080]{0,1:T(8,128)(2,1)S(1)}, bf16[128,2080]{0,1:T(8,128)(2,1)}, u32[]{:S(2)}) copy-start(bf16[128,2080]{0,1:T(8,128)(2,1)} %copy-done.10) | copy-start | bytes 1597444
  771.0 283.1 %all-reduce.27.cloned.1.call-start = ((), (), s32[]{:S(2)}) async-start(), calls=%async_computation.7 | async-start | bytes 4259840 | tf_op jit(solution)/shard_map/psum | solution.py:86
  885.9 1.5 copy-start.7
  887.4 1.0 copy-start.9
  888.5 1.8 copy-start.14
  890.3 163.8 %copy-start.13 = (s32[2080,256]{1,0:T(8,128)S(1)}, s32[2080,256]{1,0:T(8,128)}, u32[]{:S(2)}) copy-start(s32[2080,256]{1,0:T(8,128)} %param.11) | copy-start | bytes 6389764
Sparse Core Ops, SparseCore 0:
  22.3 118.1 all-reduce.12
  152.8 113.4 all-reduce.14
  284.1 113.4 all-reduce.16
  415.2 113.4 all-reduce.18
  534.8 113.4 all-reduce.20
  653.5 113.4 all-reduce.22
  771.1 113.4 all-reduce.24
  890.4 163.6 all-reduce.26
where the time goes:
time: 1060 us
  waiting for transfers between devices  963 us (91%)
  local copies, waits for them, and re-layouts  47.4 us (4%)
  other arithmetic  20.6 us (2%)
  matrix products  18.4 us (2%)
  between operations  14.5 us (1%)
    psum x4, waiting for transfers between devices, derive(): return lax.psum(partial_rate, 'cand')  459 us
    psum x3, waiting for transfers between devices, pullback(): return lax.psum(partial_cot, 'cand')  340 us
    psum x1, waiting for transfers between devices, body(): total = lax.psum(grad, 'traj')  163 us
    gather x8, local copies, waits for them, and re-layouts, factors(): return (jnp.take(z, left, axis=1), jnp.take(z, right, axis=1))  37.1 us
  transfers between devices with their start and end apart: 8, of which 8 were waited for; matrix products, arithmetic and copies ran while one was open for 0% of the time, Pallas kernels for 0%

commit v1 on v0

v1 whole, which is shorter than its diff:
```python
import functools
import math

import jax
import jax.numpy as jnp
from jax import lax
from jax.experimental import pallas as pl
from jax.experimental.pallas import tpu as pltpu
from jax.sharding import PartitionSpec as P

DT = 0.25
NT = (((1,), (1,)), ((), ()))
CHUNK = 1664
FULL = pl.BlockSpec(memory_space=pltpu.VMEM)


def chain_kernel(
    scale,
    segments,
    state_ref,
    target_ref,
    left_ref,
    right_ref,
    w_hbm,
    hot_hbm,
    out_ref,
    w_ref,
    hot_ref,
    zl_ref,
    zr_ref,
    u_ref,
    keep_ref,
    sems,
):
    rows, modes = state_ref.shape
    total = w_ref.shape[0]
    groups = modes // 64

    def fetch(start):
        at = pl.ds(start, CHUNK)
        return pltpu.make_async_copy(w_hbm.at[at], w_ref.at[at], sems.at[start // CHUNK])

    fetches = [fetch(start) for start in range(0, total, CHUNK)]
    for copy in fetches:
        copy.start()
    hot_copy = pltpu.make_async_copy(hot_hbm, hot_ref, sems.at[total // CHUNK])
    hot_copy.start()
    state = state_ref[...]

    def derive(y, s, waits=None):
        halves = [y[:, j : j + 128] for j in range(0, modes, 128)]

        def pick(index):
            index = jnp.broadcast_to(index, (rows, 128))
            lane = index & 127
            value = jnp.ones((rows, 128), jnp.float32)
            for j in reversed(range(len(halves))):
                value = jnp.where(index < 128 * (j + 1), jnp.take_along_axis(halves[j], lane, axis=1), value)
            return value

        acc = jnp.zeros((rows, modes), jnp.float32)
        for start in range(0, total, CHUNK):
            parts = []
            for j in range(start, start + CHUNK, 128):
                zl, zr = pick(left_ref[0:1, j : j + 128]), pick(right_ref[0:1, j : j + 128])
                zl_ref[s, :, j : j + 128] = zl
                zr_ref[s, :, j : j + 128] = zr
                parts.append((zl * zr).astype(jnp.bfloat16))
            theta = jnp.concatenate(parts, axis=1)
            if waits is not None:
                waits[start // CHUNK].wait()
            acc = acc + jnp.dot(theta, w_ref[start : start + CHUNK, :], preferred_element_type=jnp.float32)
        return scale * acc

    def pull(g, s):
        g16 = g.astype(jnp.bfloat16)
        for start in range(0, total, CHUNK):
            w = w_ref[start : start + CHUNK, :]
            h = scale * lax.dot_general(g16, w, NT, preferred_element_type=jnp.float32)
            for j in range(0, CHUNK, 128):
                at = slice(start + j, start + j + 128)
                pieces = []
                for index_ref, z_ref in ((left_ref, zr_ref), (right_ref, zl_ref)):
                    u = h[:, j : j + 128] * z_ref[s, :, at]
                    group = jnp.broadcast_to(index_ref[0:1, at], (rows, 128)) >> 6
                    pieces += [jnp.where(group == a, u, 0.0) for a in range(groups)]
                u_ref[:, at] = jnp.concatenate(pieces, 0).astype(jnp.bfloat16)
        acc = jnp.dot(u_ref[...], hot_ref[...], preferred_element_type=jnp.float32)
        half = groups * rows
        left = [acc[a * rows : (a + 1) * rows, :64] for a in range(groups)]
        right = [acc[half + a * rows : half + (a + 1) * rows, 64:] for a in range(groups)]
        return jnp.concatenate(left, 1) + jnp.concatenate(right, 1)

    k1 = derive(state, 0, fetches)
    keep_ref[0] = state
    keep_ref[1] = state + 0.5 * DT * k1

    def section(s, total_slope):
        k = derive(keep_ref[s], s)

        @pl.when(s < 3)
        def _():
            keep_ref[s + 1] = state + jnp.where(s == 2, DT, 0.5 * DT) * k

        return total_slope + jnp.where(s == 3, 1.0, 2.0) * k

    slope = lax.fori_loop(1, 4, section, k1) / 6.0
    a = (state + DT * slope - target_ref[...]) / segments
    keep_ref[7] = DT / 6.0 * a
    hot_copy.wait()

    def back(t, carry):
        s = 3 - t
        c = pull(keep_ref[4 + s], s)
        keep_ref[3 + s] = jnp.where(s == 1, DT / 6.0, DT / 3.0) * a + jnp.where(s == 3, DT, 0.5 * DT) * c
        return carry

    lax.fori_loop(0, 3, back, 0)
    high = slope.astype(jnp.bfloat16).astype(jnp.float32)
    packed = jnp.concatenate([keep_ref[i] for i in range(8)] + [high, slope - high], 0).astype(jnp.bfloat16)
    for d in range(out_ref.shape[0]):
        out_ref[d] = packed


def run_chain(state, target, left, right, coeffs, hot, copies, segments):
    total, modes = coeffs.shape
    rows = state.shape[0]
    return pl.pallas_call(
        functools.partial(chain_kernel, 1.0 / math.sqrt(total), segments),
        out_shape=jax.ShapeDtypeStruct((copies, 10 * rows, modes), jnp.bfloat16),
        in_specs=[FULL] * 4 + [pl.BlockSpec(memory_space=pl.ANY)] * 2,
        out_specs=FULL,
        scratch_shapes=[
            pltpu.VMEM((total, modes), jnp.bfloat16),
            pltpu.VMEM((total, 128), jnp.bfloat16),
            pltpu.VMEM((4, rows, total), jnp.float32),
            pltpu.VMEM((4, rows, total), jnp.float32),
            pltpu.VMEM((2 * (modes // 64) * rows, total), jnp.bfloat16),
            pltpu.VMEM((8, rows, modes), jnp.float32),
            pltpu.SemaphoreType.DMA((total // CHUNK + 1,)),
        ],
        compiler_params=pltpu.CompilerParams(vmem_limit_bytes=56 * 2**20),
        name="chain",
    )(state, target, left, right, coeffs, hot)


def grad_kernel(scale, block, packed_ref, left_ref, right_ref, consts_ref, out_ref):
    count, height, modes = packed_ref.shape
    rows = height // 10
    y = packed_ref[:, : 4 * rows, :].reshape(count * 4 * rows, modes)
    g = packed_ref[:, 4 * rows : 8 * rows, :].reshape(count * 4 * rows, modes)
    cands = left_ref.shape[0]
    for start in range(0, cands, block):
        at = slice(start, start + block)
        zl = lax.dot_general(left_ref[at, :], y, NT, preferred_element_type=jnp.float32) + consts_ref[at, 0:1]
        zr = lax.dot_general(right_ref[at, :], y, NT, preferred_element_type=jnp.float32) + consts_ref[at, 1:2]
        theta = (zl * zr).astype(jnp.bfloat16)
        grad = scale * jnp.dot(theta, g, preferred_element_type=jnp.float32)
        out_ref[at, :] = grad.astype(jnp.bfloat16)
    rest = out_ref.shape[0] - cands
    out_ref[cands:, :] = jnp.zeros((rest, modes), jnp.bfloat16)


def run_grad(packed, left, right, consts, total, height):
    modes = packed.shape[2]
    return pl.pallas_call(
        functools.partial(grad_kernel, 1.0 / math.sqrt(total), 416),
        out_shape=jax.ShapeDtypeStruct((height, modes), jnp.bfloat16),
        in_specs=[FULL] * 4,
        out_specs=FULL,
        compiler_params=pltpu.CompilerParams(vmem_limit_bytes=32 * 2**20),
        name="grad",
    )(packed, left, right, consts)


def body(state, target, coeffs, pairs, mask):
    block_rows, modes = state.shape
    own = coeffs.shape[0]
    n_traj, n_cand = lax.axis_size("traj"), lax.axis_size("cand")
    segments, total = block_rows * n_traj, own * n_cand
    rows = block_rows // n_cand
    start = lax.axis_index("cand") * rows

    weights = lax.all_gather(coeffs, "cand", axis=0, tiled=True)
    index = lax.all_gather(pairs, "cand", axis=1, tiled=True)
    state_own = lax.dynamic_slice_in_dim(state, start, rows, 0)
    target_own = lax.dynamic_slice_in_dim(target, start, rows, 0)
    mode = jnp.arange(modes, dtype=jnp.int32)
    left_hot = (pairs[0][:, None] == mode[None, :]).astype(jnp.bfloat16)
    right_hot = (pairs[1][:, None] == mode[None, :]).astype(jnp.bfloat16)
    consts = (pairs.T == modes).astype(jnp.float32)
    piece = -(-own // (8 * n_traj)) * 8
    height = piece * n_traj
    at = lax.axis_index("traj") * piece
    fill = ((0, height - own), (0, 0))
    coeffs_piece = lax.dynamic_slice_in_dim(jnp.pad(coeffs, fill), at, piece, 0).astype(jnp.float32)
    mask_piece = lax.dynamic_slice_in_dim(jnp.pad(mask, fill), at, piece, 0).astype(jnp.float32)

    lane = jnp.arange(128, dtype=jnp.int32)[None, :]
    low = jnp.where(lane < 64, index[0][:, None], index[1][:, None]) & 63
    hot = (low == (lane & 63)).astype(jnp.bfloat16)

    packed = run_chain(state_own, target_own, index[0:1], index[1:2], weights, hot, n_cand, segments)
    packed = lax.all_to_all(packed, "cand", 0, 0, tiled=True)
    tail = packed[:, 8 * rows :, :].astype(jnp.float32)
    slope = (tail[:, :rows] + tail[:, rows:]).reshape(block_rows, modes)

    grad = run_grad(packed, left_hot, right_hot, consts, total, height)
    grad = lax.all_to_all(grad.reshape(n_traj, piece, modes), "traj", 0, 0, tiled=True)
    grad = jnp.sum(grad.astype(jnp.float32), axis=0)
    rate = 0.5 * math.sqrt(segments * total) / DT
    fresh = (mask_piece * (coeffs_piece - rate * grad)).astype(jnp.bfloat16)
    fresh = jnp.broadcast_to(fresh[None], (n_traj, piece, modes))
    fresh = lax.all_to_all(fresh, "traj", 0, 0, tiled=True)
    return slope, fresh.reshape(height, modes)[:own]


def solution(mesh):
    placed = (P("traj", None), P("traj", None), P("cand", None), P(None, "cand"), P("cand", None))
    return jax.shard_map(
        body,
        mesh=mesh,
        in_specs=placed,
        out_specs=(P("traj", None), P("cand", None)),
        check_vma=False,
    )
```

time: 1060 us -> 267 us (0.25)
  waiting for transfers between devices: 963 us -> 137 us
  local copies, waits for them, and re-layouts: 47.4 us -> 5.41 us
  Pallas kernels: 0 us -> 39.8 us
  blocking collectives: 0 us -> 24.2 us
  starting transfers between devices: 0.51 us -> 20.1 us
  matrix products: 18.4 us -> 0 us
    psum x8 -> x0, waiting for transfers between devices: 962 us -> none  [the longest x4 459 us: derive(): return lax.psum(partial_rate, 'cand')]
    all_to_all x0 -> x3, waiting for transfers between devices: none -> 78.1 us  [the longest x1 32 us: body(): lax.all_to_all(grad.reshape(n_traj, piece, modes), 'traj', 0, 0, tiled=True)]
    all_gather x0 -> x1, waiting for transfers between devices: none -> 58.4 us  [body(): weights = lax.all_gather(coeffs, 'cand', axis=0, tiled=True)]
    pallas_call x0 -> x2, Pallas kernels: none -> 39.8 us  [the longest x1 35.6 us: run_chain(): pl.pallas_call(functools.partial(chain_kernel, 1.0 / math.sqrt(total), se...]
    gather x8 -> x0, local copies, waits for them, and re-layouts: 37.1 us -> none  [factors(): return (jnp.take(z, left, axis=1), jnp.take(z, right, axis=1))]
    all_gather x0 -> x1, blocking collectives: none -> 24.2 us  [body(): index = lax.all_gather(pairs, 'cand', axis=1, tiled=True)]
    all_to_all x0 -> x3, starting transfers between devices: none -> 20 us  [the longest x1 9.98 us: body(): lax.all_to_all(grad.reshape(n_traj, piece, modes), 'traj', 0, 0, tiled=True)]
    dot_general x17 -> x0, matrix products: 18.4 us -> none  [the longest x4 5.03 us: outer(): lax.dot_general(theta, grad_cot.astype(jnp.bfloat16), (((0,), (0,)), ((),...]
  transfers between devices with their start and end apart: 8 -> 4, of which waited for: 8 -> 4; matrix products, arithmetic and copies ran while one was open for 0% -> 10% of each run, Pallas kernels for 0% -> 0%
where the time goes in v1:
time: 267 us; the launch traced here: 266 us
  waiting for transfers between devices  137 us (51%)
  Pallas kernels  39.8 us (15%)
  other arithmetic  25.4 us (10%)
  blocking collectives  24.2 us (9%)
  starting transfers between devices  20.1 us (8%)
  between operations  14.1 us (5%)
  local copies, waits for them, and re-layouts  5.41 us (2%)
    all_gather x1, waiting for transfers between devices, body(): weights = lax.all_gather(coeffs, 'cand', axis=0, tiled=True)  58.4 us
    pallas_call x1, Pallas kernels, run_chain(): pl.pallas_call(functools.partial(chain_kernel, 1.0 / math.sqrt(total), se...  35.6 us
    all_to_all x1, waiting for transfers between devices, body(): lax.all_to_all(grad.reshape(n_traj, piece, modes), 'traj', 0, 0, tiled=True)  32 us
    all_to_all x1, waiting for transfers between devices, body(): fresh = lax.all_to_all(fresh, 'traj', 0, 0, tiled=True)  29.7 us
    all_gather x1, blocking collectives, body(): index = lax.all_gather(pairs, 'cand', axis=1, tiled=True)  24.2 us
    convert_element_type x1, other arithmetic, body(): hot = (low == lane & 63).astype(jnp.bfloat16)  21.4 us
    all_to_all x1, waiting for transfers between devices, body(): packed = lax.all_to_all(packed, 'cand', 0, 0, tiled=True)  16.4 us
    all_to_all x1, starting transfers between devices, body(): lax.all_to_all(grad.reshape(n_traj, piece, modes), 'traj', 0, 0, tiled=True)  9.98 us
  transfers between devices with their start and end apart: 4, of which 4 were waited for; matrix products, arithmetic and copies ran while one was open for 10% of the time, Pallas kernels for 0%

profile of v1, /device:TPU:8, one launch (start us, length us, event | category | flops | bytes accessed | tf_op | source)
XLA Modules:
  0.0 266.2 jit_solution(10543797024904535562)
XLA Ops:
  7.2 0.0 all-gather.3.cloned.1.call-start
  7.2 0.7 all-gather.3.cloned.1.call-update
  7.9 24.2 %all-gather = s32[16,2080,2]{1,2,0:T(2,128)S(1)} all-gather(s32[1,2080,2]{1,2,0:T(2,128)} %bitcast.14), channel_id=1, replica_groups=mesh['traj'=32,'cand'=16] {'cand'}, dimensions={0}, use_global_device_ids=true | all-gather | bytes 282880 | tf_op jit(solution)/shard_map/all_gather | solution.py:185
  32.1 0.3 reshape.32
  32.4 1.3 constant_dynamic-slice_fusion
  33.8 1.2 slice_reduce_fusion.3
  35.0 21.4 %fusion.hot_hbm = bf16[33280,128]{1,0:T(8,128)(2,1)} fusion(s32[128]{0:T(128)S(1)} %iota_and_fusion, s32[33280]{0:T(1024)S(1)} %get-tuple-element.3, s32[33280]{0:T(1024)S(1)} %get-tuple-element.2, pred[128]{0:T(512)(128)(4,1)S(1)} %iota_compare_fusion.2), kind=kLoop, calls=%fused_computation.1 | loop fusion | flops 17039360 | bytes 8786560 | tf_op jit(solution)/shard_map/convert_element_type | solution.py:201
  56.4 58.4 %all-gather.3.cloned.1.call-done.w_hbm = bf16[33280,256]{1,0:T(8,128)(2,1)} async-done(((bf16[2080,256]{1,0:T(8,128)(2,1)}), bf16[33280,256]{1,0:T(8,128)(2,1)}) %all-gather.3.cloned.1.call-update) | async-done | bytes 17039376 | tf_op jit(solution)/shard_map/all_gather | solution.py:184
  114.8 0.0 copy-start.1
  114.8 35.6 %chain.1 = bf16[16,80,256]{2,1,0:T(8,128)(2,1)} custom-call(f32[8,256]{1,0:T(8,128)} %get-tuple-element.9.state_ref, f32[8,256]{1,0:T(8,128)} %get-tuple-element.8.target_ref, s32[1,33280]{1,0:T(1,128)} %get-tuple-element.7.left_ref, s32[1,33280]{1,0:T(1,128)} %get-tuple-element.6.right_ref, bf16[33280,256]{1,0:T(8,128)(2,1)} %all-gather.3.cloned.1.call-done.w_hbm, ...), custom_call_target="tpu_custom_call" | custom-call | tf_op jit(solution)/shard_map/chain/pallas_call | solution.py:128
  150.4 4.4 %all-to-all-start = ((bf16[16,80,256]{2,1,0:T(8,128)(2,1)}), bf16[16,80,256]{2,1,0:T(8,128)(2,1)}, u32[]{:S(2)}, u32[]{:S(2)}) async-start(bf16[16,80,256]{2,1,0:T(8,128)(2,1)} %chain.1), calls=%async_computation | async-start | bytes 1310720 | tf_op jit(solution)/shard_map/all_to_all | solution.py:204
  154.9 0.0 copy-done.1
  154.9 0.4 copy.14
  155.3 0.1 slice_reduce_fusion
  155.3 1.2 fusion.1
  156.6 16.4 %all-to-all-done.packed_ref = bf16[16,80,256]{2,1,0:T(8,128)(2,1)} async-done(((bf16[16,80,256]{2,1,0:T(8,128)(2,1)}), bf16[16,80,256]{2,1,0:T(8,128)(2,1)}, u32[]{:S(2)}, u32[]{:S(2)}) %all-to-all-start) | async-done | bytes 655392 | tf_op jit(solution)/shard_map/all_to_all | solution.py:204
  173.0 4.1 %grad.1 = bf16[2304,256]{1,0:T(8,128)(2,1)} custom-call(bf16[16,80,256]{2,1,0:T(8,128)(2,1)} %all-to-all-done.packed_ref, bf16[2080,256]{1,0:T(8,128)(2,1)S(1)} %get-tuple-element.10.left_ref, bf16[2080,256]{1,0:T(8,128)(2,1)S(1)} %get-tuple-element.11.right_ref, f32[2080,2]{1,0:T(8,128)S(1)} %bitcast.11), custom_call_target="tpu_custom_call" | custom-call | tf_op jit(solution)/shard_map/grad/pallas_call | solution.py:166
  177.2 0.0 copy-start
  177.2 10.0 %all-to-all-start.1 = ((bf16[32,72,256]{2,1,0:T(8,128)(2,1)}), bf16[32,72,256]{2,1,0:T(8,128)(2,1)S(1)}, u32[]{:S(2)}, u32[]{:S(2)}) async-start(bf16[32,72,256]{2,1,0:T(8,128)(2,1)} %bitcast.5), calls=%async_computation.1 | async-start | bytes 2359296 | tf_op jit(solution)/shard_map/all_to_all | solution.py:209
  187.1 32.0 %all-to-all-done.1 = bf16[32,72,256]{2,1,0:T(8,128)(2,1)S(1)} async-done(((bf16[32,72,256]{2,1,0:T(8,128)(2,1)}), bf16[32,72,256]{2,1,0:T(8,128)(2,1)S(1)}, u32[]{:S(2)}, u32[]{:S(2)}) %all-to-all-start.1) | async-done | bytes 1179680 | tf_op jit(solution)/shard_map/all_to_all | solution.py:209
  219.1 0.2 convert_reduce_fusion
  219.3 0.0 copy-done
  219.3 0.9 multiply_convert_fusion
  220.2 1.1 broadcast_in_dim.42
  221.3 5.6 %all-to-all-start.2 = ((bf16[32,72,256]{2,1,0:T(8,128)(2,1)}), bf16[32,72,256]{2,1,0:T(8,128)(2,1)S(1)}, u32[]{:S(2)}, u32[]{:S(2)}) async-start(bf16[32,72,256]{2,1,0:T(8,128)(2,1)} %broadcast_in_dim.42), calls=%async_computation.2 | async-start | bytes 2359296 | tf_op jit(solution)/shard_map/all_to_all | solution.py:214
  226.9 0.9 slice_convert_fusion
  227.9 0.7 fusion.3
  228.5 29.7 %all-to-all-done.2 = bf16[32,72,256]{2,1,0:T(8,128)(2,1)S(1)} async-done(((bf16[32,72,256]{2,1,0:T(8,128)(2,1)}), bf16[32,72,256]{2,1,0:T(8,128)(2,1)S(1)}, u32[]{:S(2)}, u32[]{:S(2)}) %all-to-all-start.2) | async-done | bytes 1179680 | tf_op jit(solution)/shard_map/all_to_all | solution.py:214
  258.3 1.0 slice.39
  (4 shorter events, 0.0 us)
Async XLA Ops:
  7.2 107.6 %all-gather.3.cloned.1.call-start = ((), (), s32[]{:S(2)}) async-start(), calls=%async_computation.3 | async-start | bytes 18104320 | tf_op jit(solution)/shard_map/all_gather | solution.py:184
  114.8 40.1 %copy-start.1 = (s32[2,2080]{1,0:T(2,128)S(1)}, s32[2,2080]{1,0:T(2,128)}, u32[]{:S(2)}) copy-start(s32[2,2080]{1,0:T(2,128)} %param.8) | copy-start | bytes 49924
  150.4 22.6 %all-to-all-start = ((bf16[16,80,256]{2,1,0:T(8,128)(2,1)}), bf16[16,80,256]{2,1,0:T(8,128)(2,1)}, u32[]{:S(2)}, u32[]{:S(2)}) async-start(bf16[16,80,256]{2,1,0:T(8,128)(2,1)} %chain.1), calls=%async_computation | async-start | bytes 1310720 | tf_op jit(solution)/shard_map/all_to_all | solution.py:204
  177.2 42.1 %copy-start = (bf16[2080,256]{1,0:T(8,128)(2,1)S(1)}, bf16[2080,256]{1,0:T(8,128)(2,1)}, u32[]{:S(2)}) copy-start(bf16[2080,256]{1,0:T(8,128)(2,1)} %param.7) | copy-start | bytes 3194884
  177.2 42.0 %all-to-all-start.1 = ((bf16[32,72,256]{2,1,0:T(8,128)(2,1)}), bf16[32,72,256]{2,1,0:T(8,128)(2,1)S(1)}, u32[]{:S(2)}, u32[]{:S(2)}) async-start(bf16[32,72,256]{2,1,0:T(8,128)(2,1)} %bitcast.5), calls=%async_computation.1 | async-start | bytes 2359296 | tf_op jit(solution)/shard_map/all_to_all | solution.py:209
  221.3 37.0 %all-to-all-start.2 = ((bf16[32,72,256]{2,1,0:T(8,128)(2,1)}), bf16[32,72,256]{2,1,0:T(8,128)(2,1)S(1)}, u32[]{:S(2)}, u32[]{:S(2)}) async-start(bf16[32,72,256]{2,1,0:T(8,128)(2,1)} %broadcast_in_dim.42), calls=%async_computation.2 | async-start | bytes 2359296 | tf_op jit(solution)/shard_map/all_to_all | solution.py:214
Sparse Core Ops, SparseCore 0:
  10.1 104.6 all-gather.2

commit v2 on v1

--- a/solution.py
+++ b/solution.py
@@ -6,11 +6,12 @@
 from jax import lax
 from jax.experimental import pallas as pl
 from jax.experimental.pallas import tpu as pltpu
-from jax.sharding import PartitionSpec as P
+from jax.sharding import Mesh, PartitionSpec as P
 
 DT = 0.25
 NT = (((1,), (1,)), ((), ()))
 CHUNK = 1664
+AXES = ("x", "y", "z", "c")
 FULL = pl.BlockSpec(memory_space=pltpu.VMEM)
 
 
@@ -116,8 +117,7 @@
         return carry
 
     lax.fori_loop(0, 3, back, 0)
-    high = slope.astype(jnp.bfloat16).astype(jnp.float32)
-    packed = jnp.concatenate([keep_ref[i] for i in range(8)] + [high, slope - high], 0).astype(jnp.bfloat16)
+    packed = jnp.concatenate([slope] + [keep_ref[i] for i in range(1, 8)], 0).astype(jnp.bfloat16)
     for d in range(out_ref.shape[0]):
         out_ref[d] = packed
 
@@ -127,7 +127,7 @@
     rows = state.shape[0]
     return pl.pallas_call(
         functools.partial(chain_kernel, 1.0 / math.sqrt(total), segments),
-        out_shape=jax.ShapeDtypeStruct((copies, 10 * rows, modes), jnp.bfloat16),
+        out_shape=jax.ShapeDtypeStruct((copies, 8 * rows, modes), jnp.bfloat16),
         in_specs=[FULL] * 4 + [pl.BlockSpec(memory_space=pl.ANY)] * 2,
         out_specs=FULL,
         scratch_shapes=[
@@ -144,11 +144,16 @@
     )(state, target, left, right, coeffs, hot)
 
 
-def grad_kernel(scale, block, packed_ref, left_ref, right_ref, consts_ref, out_ref):
-    count, height, modes = packed_ref.shape
-    rows = height // 10
-    y = packed_ref[:, : 4 * rows, :].reshape(count * 4 * rows, modes)
-    g = packed_ref[:, 4 * rows : 8 * rows, :].reshape(count * 4 * rows, modes)
+def grad_kernel(scale, block, first_ref, mine_ref, other_ref, left_ref, right_ref, consts_ref, out_ref):
+    count, height, modes = mine_ref.shape
+    rows = height // 8
+    ys, gs = [], []
+    for core, ref in enumerate((mine_ref, other_ref)):
+        values = ref[...].astype(jnp.float32)
+        y = jnp.concatenate([first_ref[core], values[:, rows : 4 * rows]], 1)
+        ys.append(y.reshape(count * 4 * rows, modes).astype(jnp.bfloat16))
+        gs.append(values[:, 4 * rows :].reshape(count * 4 * rows, modes).astype(jnp.bfloat16))
+    y, g = jnp.concatenate(ys, 0), jnp.concatenate(gs, 0)
     cands = left_ref.shape[0]
     for start in range(0, cands, block):
         at = slice(start, start + block)
@@ -161,66 +166,85 @@
     out_ref[cands:, :] = jnp.zeros((rest, modes), jnp.bfloat16)
 
 
-def run_grad(packed, left, right, consts, total, height):
-    modes = packed.shape[2]
+def run_grad(first, mine, other, left, right, consts, total, height):
+    modes = mine.shape[2]
     return pl.pallas_call(
         functools.partial(grad_kernel, 1.0 / math.sqrt(total), 416),
         out_shape=jax.ShapeDtypeStruct((height, modes), jnp.bfloat16),
-        in_specs=[FULL] * 4,
+        in_specs=[FULL] * 6,
         out_specs=FULL,
         compiler_params=pltpu.CompilerParams(vmem_limit_bytes=32 * 2**20),
         name="grad",
-    )(packed, left, right, consts)
+    )(first, mine, other, left, right, consts)
+
+
+def exchange(blocks, axis):
+    return lax.all_to_all(blocks, axis, 0, 0, tiled=True)
+
+
+def spread(block, axis):
+    count = lax.axis_size(axis)
+    blocks = exchange(jnp.broadcast_to(block[None], (count, *block.shape)), axis)
+    return blocks.reshape(count * block.shape[0], *block.shape[1:])
 
 
 def body(state, target, coeffs, pairs, mask):
     block_rows, modes = state.shape
     own = coeffs.shape[0]
-    n_traj, n_cand = lax.axis_size("traj"), lax.axis_size("cand")
-    segments, total = block_rows * n_traj, own * n_cand
-    rows = block_rows // n_cand
-    start = lax.axis_index("cand") * rows
-
-    weights = lax.all_gather(coeffs, "cand", axis=0, tiled=True)
-    index = lax.all_gather(pairs, "cand", axis=1, tiled=True)
+    nx, ny, nz, nc = [lax.axis_size(axis) for axis in AXES]
+    segments, total = block_rows * nx * ny, own * nz * nc
+    rows = block_rows // (nz * nc)
+    core = lax.axis_index("c")
+    start = lax.axis_index(("z", "c")) * rows
+
+    weights = lax.all_gather(coeffs, ("z", "c"), axis=0, tiled=True)
+    index = lax.all_gather(pairs, ("z", "c"), axis=1, tiled=True)
     state_own = lax.dynamic_slice_in_dim(state, start, rows, 0)
     target_own = lax.dynamic_slice_in_dim(target, start, rows, 0)
+    lane = jnp.arange(128, dtype=jnp.int32)[None, :]
+    low = jnp.where(lane < 64, index[0][:, None], index[1][:, None]) & 63
+    hot = (low == (lane & 63)).astype(jnp.bfloat16)
     mode = jnp.arange(modes, dtype=jnp.int32)
     left_hot = (pairs[0][:, None] == mode[None, :]).astype(jnp.bfloat16)
     right_hot = (pairs[1][:, None] == mode[None, :]).astype(jnp.bfloat16)
     consts = (pairs.T == modes).astype(jnp.float32)
-    piece = -(-own // (8 * n_traj)) * 8
-    height = piece * n_traj
-    at = lax.axis_index("traj") * piece
+    by_core = state.reshape(nz, nc, rows, modes)
+    first = jnp.where(core == 0, by_core[:, 0], by_core[:, 1]), jnp.where(core == 0, by_core[:, 1], by_core[:, 0])
+    first = jnp.stack(first)
+    piece = -(-own // (8 * nx * ny)) * 8
+    height = piece * nx * ny
+    at = lax.axis_index(("x", "y")) * piece
     fill = ((0, height - own), (0, 0))
     coeffs_piece = lax.dynamic_slice_in_dim(jnp.pad(coeffs, fill), at, piece, 0).astype(jnp.float32)
     mask_piece = lax.dynamic_slice_in_dim(jnp.pad(mask, fill), at, piece, 0).astype(jnp.float32)
 
-    lane = jnp.arange(128, dtype=jnp.int32)[None, :]
-    low = jnp.where(lane < 64, index[0][:, None], index[1][:, None]) & 63
-    hot = (low == (lane & 63)).astype(jnp.bfloat16)
-
-    packed = run_chain(state_own, target_own, index[0:1], index[1:2], weights, hot, n_cand, segments)
-    packed = lax.all_to_all(packed, "cand", 0, 0, tiled=True)
-    tail = packed[:, 8 * rows :, :].astype(jnp.float32)
-    slope = (tail[:, :rows] + tail[:, rows:]).reshape(block_rows, modes)
-
-    grad = run_grad(packed, left_hot, right_hot, consts, total, height)
-    grad = lax.all_to_all(grad.reshape(n_traj, piece, modes), "traj", 0, 0, tiled=True)
+    packed = run_chain(state_own, target_own, index[0:1], index[1:2], weights, hot, nz, segments)
+    mine = exchange(packed, "z")
+    other = lax.ppermute(mine, "c", [(0, 1), (1, 0)])
+    grad = run_grad(first, mine, other, left_hot, right_hot, consts, total, height)
+
+    slopes = [block[:, :rows].astype(jnp.float32) for block in (mine, other)]
+    slope = jnp.stack([jnp.where(core == 0, *slopes), jnp.where(core == 0, *slopes[::-1])], 1)
+    slope = slope.reshape(block_rows, modes)
+
+    grad = exchange(grad.reshape(nx, ny * piece, modes), "x")
+    grad = jnp.sum(grad.astype(jnp.float32), axis=0).astype(jnp.bfloat16)
+    grad = exchange(grad.reshape(ny, piece, modes), "y")
     grad = jnp.sum(grad.astype(jnp.float32), axis=0)
     rate = 0.5 * math.sqrt(segments * total) / DT
     fresh = (mask_piece * (coeffs_piece - rate * grad)).astype(jnp.bfloat16)
-    fresh = jnp.broadcast_to(fresh[None], (n_traj, piece, modes))
-    fresh = lax.all_to_all(fresh, "traj", 0, 0, tiled=True)
-    return slope, fresh.reshape(height, modes)[:own]
+    fresh = spread(spread(fresh, "y"), "x")
+    return slope, fresh[:own]
 
 
 def solution(mesh):
-    placed = (P("traj", None), P("traj", None), P("cand", None), P(None, "cand"), P("cand", None))
+    devices = mesh.devices.reshape(4, 8, 8, 2)
+    traj, cand = ("x", "y"), ("z", "c")
+    placed = (P(traj, None), P(traj, None), P(cand, None), P(None, cand), P(cand, None))
     return jax.shard_map(
         body,
-        mesh=mesh,
+        mesh=Mesh(devices, AXES),
         in_specs=placed,
-        out_specs=(P("traj", None), P("cand", None)),
+        out_specs=(P(traj, None), P(cand, None)),
         check_vma=False,
     )

time: 267 us -> 252 us (0.944)
  waiting for transfers between devices: 137 us -> 92.2 us
  blocking collectives: 24.2 us -> 58.3 us
  starting transfers between devices: 20.1 us -> 16.8 us
    all_to_all x3, waiting for transfers between devices: 78.1 us -> 32.9 us  [exchange(): return lax.all_to_all(blocks, axis, 0, 0, tiled=True)]
    all_to_all x0 -> x2, blocking collectives: none -> 34.2 us  [exchange(): return lax.all_to_all(blocks, axis, 0, 0, tiled=True)]
    all_to_all x3, starting transfers between devices: 20 us -> 14.8 us  [exchange(): return lax.all_to_all(blocks, axis, 0, 0, tiled=True)]
  transfers between devices with their start and end apart: 4 -> 5, of which waited for: 4 -> 5; matrix products, arithmetic and copies ran while one was open for 10% -> 11% of each run, Pallas kernels for 0% -> 0%
where the time goes in v2:
time: 252 us; the launch traced here: 251 us
  waiting for transfers between devices  92.2 us (37%)
  blocking collectives  58.3 us (23%)
  Pallas kernels  37.5 us (15%)
  other arithmetic  26.2 us (10%)
  starting transfers between devices  16.8 us (7%)
  between operations  14.2 us (6%)
  local copies, waits for them, and re-layouts  6.1 us (2%)
    all_gather x1, waiting for transfers between devices, body(): weights = lax.all_gather(coeffs, ('z', 'c'), axis=0, tiled=True)  58 us
    pallas_call x1, Pallas kernels, run_chain(): pl.pallas_call(functools.partial(chain_kernel, 1.0 / math.sqrt(total), se...  35.5 us
    all_to_all x2, blocking collectives, exchange(): return lax.all_to_all(blocks, axis, 0, 0, tiled=True)  34.2 us
    all_to_all x3, waiting for transfers between devices, exchange(): return lax.all_to_all(blocks, axis, 0, 0, tiled=True)  32.9 us
    all_gather x1, blocking collectives, body(): index = lax.all_gather(pairs, ('z', 'c'), axis=1, tiled=True)  24.2 us
    convert_element_type x1, other arithmetic, body(): hot = (low == lane & 63).astype(jnp.bfloat16)  21.4 us
    all_to_all x3, starting transfers between devices, exchange(): return lax.all_to_all(blocks, axis, 0, 0, tiled=True)  14.8 us
  transfers between devices with their start and end apart: 5, of which 5 were waited for; matrix products, arithmetic and copies ran while one was open for 11% of the time, Pallas kernels for 0%

profile of v2, /device:TPU:8, one launch (start us, length us, event | category | flops | bytes accessed | tf_op | source)
XLA Modules:
  0.0 251.3 jit_solution(8559074950724935075)
XLA Ops:
  7.2 0.0 copy-start.2
  7.2 0.0 all-gather.3.cloned.1.call-start
  7.2 0.7 all-gather.3.cloned.1.call-update
  7.9 24.2 %all-gather = s32[16,2080,2]{1,2,0:T(2,128)S(1)} all-gather(s32[1,2080,2]{1,2,0:T(2,128)} %bitcast.38), channel_id=1, replica_groups=mesh['x'=4,'y'=8,'z'=8,'c'=2] {'z','c'}, dimensions={0}, use_global_device_ids=true | all-gather | bytes 282880 | tf_op jit(solution)/shard_map/all_gather | solution.py:201
  32.1 0.3 reshape.79
  32.4 0.0 copy-done.2
  32.5 0.4 copy.32
  32.9 1.3 constant_dynamic-slice_fusion
  34.2 1.2 slice_reduce_fusion.3
  35.4 21.4 %fusion.hot_hbm = bf16[33280,128]{1,0:T(8,128)(2,1)} fusion(s32[128]{0:T(128)S(1)} %iota_and_fusion, s32[33280]{0:T(1024)S(1)} %get-tuple-element.3, s32[33280]{0:T(1024)S(1)} %get-tuple-element.2, pred[128]{0:T(512)(128)(4,1)S(1)} %iota_compare_fusion.2), kind=kLoop, calls=%fused_computation.1 | loop fusion | flops 17039360 | bytes 8786560 | tf_op jit(solution)/shard_map/convert_element_type | solution.py:206
  56.8 58.0 %all-gather.3.cloned.1.call-done.w_hbm = bf16[33280,256]{1,0:T(8,128)(2,1)} async-done(((bf16[2080,256]{1,0:T(8,128)(2,1)}), bf16[33280,256]{1,0:T(8,128)(2,1)}) %all-gather.3.cloned.1.call-update) | async-done | bytes 17039376 | tf_op jit(solution)/shard_map/all_gather | solution.py:200
  114.8 35.5 %chain.1 = bf16[8,64,256]{2,1,0:T(8,128)(2,1)} custom-call(f32[8,256]{1,0:T(8,128)} %get-tuple-element.13.state_ref, f32[8,256]{1,0:T(8,128)} %get-tuple-element.12.target_ref, s32[1,33280]{1,0:T(1,128)} %get-tuple-element.9.left_ref, s32[1,33280]{1,0:T(1,128)} %get-tuple-element.8.right_ref, bf16[33280,256]{1,0:T(8,128)(2,1)} %all-gather.3.cloned.1.call-done.w_hbm, ...), custom_call_target="tpu_custom_call" | custom-call | tf_op jit(solution)/shard_map/chain/pallas_call | solution.py:128
  150.3 4.0 %all-to-all-start = ((bf16[8,64,256]{2,1,0:T(8,128)(2,1)}), bf16[8,64,256]{2,1,0:T(8,128)(2,1)S(1)}, u32[]{:S(2)}, u32[]{:S(2)}) async-start(bf16[8,64,256]{2,1,0:T(8,128)(2,1)} %chain.1), calls=%async_computation | async-start | bytes 524288 | tf_op jit(solution)/shard_map/all_to_all | solution.py:182
  154.3 1.2 fusion.1
  155.5 11.1 %all-to-all-done.mine_ref = bf16[8,64,256]{2,1,0:T(8,128)(2,1)S(1)} async-done(((bf16[8,64,256]{2,1,0:T(8,128)(2,1)}), bf16[8,64,256]{2,1,0:T(8,128)(2,1)S(1)}, u32[]{:S(2)}, u32[]{:S(2)}) %all-to-all-start) | async-done | bytes 262176 | tf_op jit(solution)/shard_map/all_to_all | solution.py:182
  166.6 1.9 collective-permute-start
  168.5 0.9 select_bitcast_fusion.1
  169.4 0.6 collective-permute-done.other_ref
  170.0 0.0 copy-start
  170.0 2.0 grad.1
  172.0 0.0 copy-done
  172.1 0.0 copy-start.1
  172.1 21.0 %all_to_all.25 = bf16[4,576,256]{2,1,0:T(8,128)(2,1)S(1)} all-to-all(bf16[4,576,256]{2,1,0:T(8,128)(2,1)S(1)} %bitcast.33), channel_id=1, replica_groups=mesh['x'=4,'y'=8,'z'=8,'c'=2] {'x'}, dimensions={0} | all-to-all | bytes 2359296 | tf_op jit(solution)/shard_map/all_to_all | solution.py:182
  193.0 0.9 reduce_sum.21
  194.0 7.3 %all-to-all-start.2 = ((bf16[8,72,256]{2,1,0:T(8,128)(2,1)}), bf16[8,72,256]{2,1,0:T(8,128)(2,1)S(1)}, u32[]{:S(2)}, u32[]{:S(2)}) async-start(bf16[8,72,256]{2,1,0:T(8,128)(2,1)} %bitcast.11), calls=%async_computation.2 | async-start | bytes 589824 | tf_op jit(solution)/shard_map/all_to_all | solution.py:182
  201.3 10.0 %all-to-all-done.2 = bf16[8,72,256]{2,1,0:T(8,128)(2,1)S(1)} async-done(((bf16[8,72,256]{2,1,0:T(8,128)(2,1)}), bf16[8,72,256]{2,1,0:T(8,128)(2,1)S(1)}, u32[]{:S(2)}, u32[]{:S(2)}) %all-to-all-start.2) | async-done | bytes 294944 | tf_op jit(solution)/shard_map/all_to_all | solution.py:182
  211.3 0.0 copy-done.1
  211.3 0.9 multiply_convert_fusion
  212.3 13.2 %all_to_all.26 = bf16[8,72,256]{2,1,0:T(8,128)(2,1)S(1)} all-to-all(bf16[8,72,256]{2,1,0:T(8,128)(2,1)S(1)} %broadcast_in_dim.49), channel_id=1, replica_groups=mesh['x'=4,'y'=8,'z'=8,'c'=2] {'y'}, dimensions={0} | all-to-all | bytes 589824 | tf_op jit(solution)/shard_map/all_to_all | solution.py:182
  225.5 1.1 broadcast_in_dim.51
  226.6 3.5 %all-to-all-start.4 = ((bf16[4,576,256]{2,1,0:T(8,128)(2,1)}), bf16[4,576,256]{2,1,0:T(8,128)(2,1)S(1)}, u32[]{:S(2)}, u32[]{:S(2)}) async-start(bf16[4,576,256]{2,1,0:T(8,128)(2,1)} %broadcast_in_dim.51), calls=%async_computation.4 | async-start | bytes 2359296 | tf_op jit(solution)/shard_map/all_to_all | solution.py:182
  230.1 0.8 fusion.3
  230.9 0.7 copy.29
  231.6 11.9 %all-to-all-done.4 = bf16[4,576,256]{2,1,0:T(8,128)(2,1)S(1)} async-done(((bf16[4,576,256]{2,1,0:T(8,128)(2,1)}), bf16[4,576,256]{2,1,0:T(8,128)(2,1)S(1)}, u32[]{:S(2)}, u32[]{:S(2)}) %all-to-all-start.4) | async-done | bytes 1179680 | tf_op jit(solution)/shard_map/all_to_all | solution.py:182
  243.5 1.0 slice.46
  (9 shorter events, 0.2 us)
Async XLA Ops:
  7.2 25.3 %copy-start.2 = (s32[2,2080]{1,0:T(2,128)S(1)}, s32[2,2080]{1,0:T(2,128)}, u32[]{:S(2)}) copy-start(s32[2,2080]{1,0:T(2,128)} %param.8) | copy-start | bytes 49924
  7.2 107.6 %all-gather.3.cloned.1.call-start = ((), (), s32[]{:S(2)}) async-start(), calls=%async_computation.5 | async-start | bytes 18104320 | tf_op jit(solution)/shard_map/all_gather | solution.py:200
  150.3 16.3 %all-to-all-start = ((bf16[8,64,256]{2,1,0:T(8,128)(2,1)}), bf16[8,64,256]{2,1,0:T(8,128)(2,1)S(1)}, u32[]{:S(2)}, u32[]{:S(2)}) async-start(bf16[8,64,256]{2,1,0:T(8,128)(2,1)} %chain.1), calls=%async_computation | async-start | bytes 524288 | tf_op jit(solution)/shard_map/all_to_all | solution.py:182
  166.6 3.4 %collective-permute-start = (bf16[8,64,256]{2,1,0:T(8,128)(2,1)S(1)}, bf16[8,64,256]{2,1,0:T(8,128)(2,1)S(1)}, u32[]{:S(2)}, u32[]{:S(2)}) collective-permute-start(bf16[8,64,256]{2,1,0:T(8,128)(2,1)S(1)} %all-to-all-done.mine_ref), channel_id=1, source_target_pairs={{0,1},{1,0},{2,3},{3,2},{4,5},{5,4},{6,7},{7,6},{8,9},{9,8},{10,11... | collective-permute-start | bytes 786440 | tf_op jit(solution)/shard_map/ppermute | solution.py:223
  170.0 2.0 copy-start
  172.1 39.3 %copy-start.1 = (bf16[2080,256]{1,0:T(8,128)(2,1)S(1)}, bf16[2080,256]{1,0:T(8,128)(2,1)}, u32[]{:S(2)}) copy-start(bf16[2080,256]{1,0:T(8,128)(2,1)} %param.7) | copy-start | bytes 3194884
  194.0 17.3 %all-to-all-start.2 = ((bf16[8,72,256]{2,1,0:T(8,128)(2,1)}), bf16[8,72,256]{2,1,0:T(8,128)(2,1)S(1)}, u32[]{:S(2)}, u32[]{:S(2)}) async-start(bf16[8,72,256]{2,1,0:T(8,128)(2,1)} %bitcast.11), calls=%async_computation.2 | async-start | bytes 589824 | tf_op jit(solution)/shard_map/all_to_all | solution.py:182
  226.6 16.9 %all-to-all-start.4 = ((bf16[4,576,256]{2,1,0:T(8,128)(2,1)}), bf16[4,576,256]{2,1,0:T(8,128)(2,1)S(1)}, u32[]{:S(2)}, u32[]{:S(2)}) async-start(bf16[4,576,256]{2,1,0:T(8,128)(2,1)} %broadcast_in_dim.51), calls=%async_computation.4 | async-start | bytes 2359296 | tf_op jit(solution)/shard_map/all_to_all | solution.py:182
Sparse Core Ops, SparseCore 0:
  10.1 104.6 all-gather.2

commit v3 on v2

--- a/solution.py
+++ b/solution.py
@@ -11,40 +11,29 @@
 DT = 0.25
 NT = (((1,), (1,)), ((), ()))
 CHUNK = 1664
+FETCH = 2048
+PIECE = 256
 AXES = ("x", "y", "z", "c")
 FULL = pl.BlockSpec(memory_space=pltpu.VMEM)
 
 
-def chain_kernel(
-    scale,
-    segments,
-    state_ref,
-    target_ref,
-    left_ref,
-    right_ref,
-    w_hbm,
-    hot_hbm,
-    out_ref,
-    w_ref,
-    hot_ref,
-    zl_ref,
-    zr_ref,
-    u_ref,
-    keep_ref,
-    sems,
-):
+def chain_kernel(scale, segments, buffers, state_ref, target_ref, left_ref, right_ref, hot_hbm, *refs):
+    blocks, (out_ref, w_ref, hot_ref, zl_ref, zr_ref, u_ref, keep_ref, sems) = refs[:buffers], refs[buffers:]
     rows, modes = state_ref.shape
     total = w_ref.shape[0]
     groups = modes // 64
 
-    def fetch(start):
-        at = pl.ds(start, CHUNK)
-        return pltpu.make_async_copy(w_hbm.at[at], w_ref.at[at], sems.at[start // CHUNK])
-
-    fetches = [fetch(start) for start in range(0, total, CHUNK)]
+    fetches, ends, base = [], [], 0
+    for block in blocks:
+        for start in range(0, block.shape[0], FETCH):
+            size = min(FETCH, block.shape[0] - start)
+            source, into = block.at[pl.ds(start, size)], w_ref.at[pl.ds(base + start, size)]
+            fetches.append(pltpu.make_async_copy(source, into, sems.at[len(fetches)]))
+            ends.append(base + start + size)
+        base += block.shape[0]
     for copy in fetches:
         copy.start()
-    hot_copy = pltpu.make_async_copy(hot_hbm, hot_ref, sems.at[total // CHUNK])
+    hot_copy = pltpu.make_async_copy(hot_hbm, hot_ref, sems.at[len(fetches)])
     hot_copy.start()
     state = state_ref[...]
 
@@ -68,8 +57,8 @@
                 zr_ref[s, :, j : j + 128] = zr
                 parts.append((zl * zr).astype(jnp.bfloat16))
             theta = jnp.concatenate(parts, axis=1)
-            if waits is not None:
-                waits[start // CHUNK].wait()
+            while waits and ends[len(fetches) - len(waits)] - FETCH < start + CHUNK:
+                waits.pop(0).wait()
             acc = acc + jnp.dot(theta, w_ref[start : start + CHUNK, :], preferred_element_type=jnp.float32)
         return scale * acc
 
@@ -92,7 +81,7 @@
         right = [acc[half + a * rows : half + (a + 1) * rows, 64:] for a in range(groups)]
         return jnp.concatenate(left, 1) + jnp.concatenate(right, 1)
 
-    k1 = derive(state, 0, fetches)
+    k1 = derive(state, 0, list(fetches))
     keep_ref[0] = state
     keep_ref[1] = state + 0.5 * DT * k1
 
@@ -122,13 +111,14 @@
         out_ref[d] = packed
 
 
-def run_chain(state, target, left, right, coeffs, hot, copies, segments):
-    total, modes = coeffs.shape
+def run_chain(state, target, left, right, hot, blocks, copies, segments):
+    total, modes = hot.shape[0], state.shape[1]
     rows = state.shape[0]
+    copies_in = sum(-(-block.shape[0] // FETCH) for block in blocks)
     return pl.pallas_call(
-        functools.partial(chain_kernel, 1.0 / math.sqrt(total), segments),
+        functools.partial(chain_kernel, 1.0 / math.sqrt(total), segments, len(blocks)),
         out_shape=jax.ShapeDtypeStruct((copies, 8 * rows, modes), jnp.bfloat16),
-        in_specs=[FULL] * 4 + [pl.BlockSpec(memory_space=pl.ANY)] * 2,
+        in_specs=[FULL] * 4 + [pl.BlockSpec(memory_space=pl.ANY)] * (1 + len(blocks)),
         out_specs=FULL,
         scratch_shapes=[
             pltpu.VMEM((total, modes), jnp.bfloat16),
@@ -137,11 +127,11 @@
             pltpu.VMEM((4, rows, total), jnp.float32),
             pltpu.VMEM((2 * (modes // 64) * rows, total), jnp.bfloat16),
             pltpu.VMEM((8, rows, modes), jnp.float32),
-            pltpu.SemaphoreType.DMA((total // CHUNK + 1,)),
+            pltpu.SemaphoreType.DMA((copies_in + 1,)),
         ],
         compiler_params=pltpu.CompilerParams(vmem_limit_bytes=56 * 2**20),
         name="chain",
-    )(state, target, left, right, coeffs, hot)
+    )(state, target, left, right, hot, *blocks)
 
 
 def grad_kernel(scale, block, first_ref, mine_ref, other_ref, left_ref, right_ref, consts_ref, out_ref):
@@ -178,6 +168,37 @@
     )(first, mine, other, left, right, consts)
 
 
+def gather_candidates(coeffs, pairs):
+    nx, nz, nc = [lax.axis_size(axis) for axis in ("x", "z", "c")]
+    cands, side = nz * nc, PIECE * nx
+    x, core = lax.axis_index("x"), lax.axis_index("c")
+    ahead = [(i, (i + 1) % nx) for i in range(nx)]
+    behind = [(i, (i - 1) % nx) for i in range(nx)]
+    swap = [(0, 1), (1, 0)]
+
+    mine = lax.all_gather(lax.dynamic_slice_in_dim(coeffs, x * PIECE, PIECE, 0), ("z", "c"), axis=0, tiled=True)
+    rest = lax.all_gather(coeffs[side:], ("z", "c"), axis=0, tiled=True)
+    half = mine.shape[0] // 2
+    part = lax.dynamic_slice_in_dim(mine, core * half, half, 0)
+    one, three = lax.ppermute(part, "x", ahead), lax.ppermute(part, "x", behind)
+    two = [lax.ppermute(one[: half // 2], "x", ahead), lax.ppermute(three[half // 2 :], "x", behind)]
+    got = [one, three, *two]
+    blocks = [rest, mine, *got, *[lax.ppermute(block, "c", swap) for block in got]]
+
+    index = lax.all_gather(pairs, ("z", "c"), axis=1, tiled=True).reshape(2, cands, -1)
+    sides = index[:, :, :side].reshape(2, cands, nx, PIECE)
+
+    def piece(away, first, count):
+        which = lax.rem(x + away, nx)
+        return lax.dynamic_slice(sides, (0, first, which, 0), (2, count, 1, PIECE)).reshape(2, count * PIECE)
+
+    order = [index[:, :, side:].reshape(2, -1), piece(0, 0, cands)]
+    for first in (core * (cands // 2), (1 - core) * (cands // 2)):
+        order += [piece(nx - 1, first, cands // 2), piece(1, first, cands // 2)]
+        order += [piece(2, first, cands // 4), piece(2, first + cands // 4, cands // 4)]
+    return blocks, jnp.concatenate(order, 1)
+
+
 def exchange(blocks, axis):
     return lax.all_to_all(blocks, axis, 0, 0, tiled=True)
 
@@ -197,8 +218,7 @@
     core = lax.axis_index("c")
     start = lax.axis_index(("z", "c")) * rows
 
-    weights = lax.all_gather(coeffs, ("z", "c"), axis=0, tiled=True)
-    index = lax.all_gather(pairs, ("z", "c"), axis=1, tiled=True)
+    blocks, index = gather_candidates(coeffs, pairs)
     state_own = lax.dynamic_slice_in_dim(state, start, rows, 0)
     target_own = lax.dynamic_slice_in_dim(target, start, rows, 0)
     lane = jnp.arange(128, dtype=jnp.int32)[None, :]
@@ -218,7 +238,7 @@
     coeffs_piece = lax.dynamic_slice_in_dim(jnp.pad(coeffs, fill), at, piece, 0).astype(jnp.float32)
     mask_piece = lax.dynamic_slice_in_dim(jnp.pad(mask, fill), at, piece, 0).astype(jnp.float32)
 
-    packed = run_chain(state_own, target_own, index[0:1], index[1:2], weights, hot, nz, segments)
+    packed = run_chain(state_own, target_own, index[0:1], index[1:2], hot, blocks, nz, segments)
     mine = exchange(packed, "z")
     other = lax.ppermute(mine, "c", [(0, 1), (1, 0)])
     grad = run_grad(first, mine, other, left_hot, right_hot, consts, total, height)

time: 252 us -> 265 us (1.052)
  starting transfers between devices: 16.8 us -> 40.1 us
  waiting for transfers between devices: 92.2 us -> 76.1 us
  local copies, waits for them, and re-layouts: 6.1 us -> 12.1 us
    all_gather x1 -> x2, waiting for transfers between devices: 58 us -> 21.8 us  [the longest x1 21.8 us: gather_candidates(): lax.all_gather(lax.dynamic_slice_in_dim(coeffs, x * PIECE, PIECE, 0), ('z...]
    ppermute x0 -> x8, starting transfers between devices: none -> 22.9 us  [the longest x4 8.84 us: gather_candidates(): lax.ppermute(block, 'c', swap)]
    ppermute x0 -> x8, waiting for transfers between devices: none -> 20 us  [the longest x1 20 us: gather_candidates(): lax.ppermute(part, 'x', ahead)]
    dynamic_slice x0 -> x5, local copies, waits for them, and re-layouts: none -> 3.27 us  [the longest x1 1.57 us: gather_candidates(): lax.dynamic_slice_in_dim(coeffs, x * PIECE, PIECE, 0)]
  transfers between devices with their start and end apart: 5 -> 14, of which waited for: 5 -> 6; matrix products, arithmetic and copies ran while one was open for 11% -> 12% of each run, Pallas kernels for 0% -> 0%
where the time goes in v3:
time: 265 us; the launch traced here: 264 us
  waiting for transfers between devices  76.1 us (29%)
  blocking collectives  57.4 us (22%)
  starting transfers between devices  40.1 us (15%)
  Pallas kernels  37.4 us (14%)
  other arithmetic  26.3 us (10%)
  between operations  14.6 us (6%)
  local copies, waits for them, and re-layouts  12.1 us (5%)
    pallas_call x1, Pallas kernels, run_chain(): pl.pallas_call(functools.partial(chain_kernel, 1.0 / math.sqrt(total), se...  35.3 us
    all_to_all x3, waiting for transfers between devices, exchange(): return lax.all_to_all(blocks, axis, 0, 0, tiled=True)  33.9 us
    all_to_all x2, blocking collectives, exchange(): return lax.all_to_all(blocks, axis, 0, 0, tiled=True)  33.1 us
    all_gather x1, blocking collectives, gather_candidates(): lax.all_gather(pairs, ('z', 'c'), axis=1, tiled=True).reshape(2, cands, -1)  24.3 us
    all_gather x1, waiting for transfers between devices, gather_candidates(): lax.all_gather(lax.dynamic_slice_in_dim(coeffs, x * PIECE, PIECE, 0), ('z...  21.8 us
    convert_element_type x1, other arithmetic, body(): hot = (low == lane & 63).astype(jnp.bfloat16)  21.5 us
    ppermute x1, waiting for transfers between devices, gather_candidates(): lax.ppermute(part, 'x', ahead)  20 us
    all_to_all x3, starting transfers between devices, exchange(): return lax.all_to_all(blocks, axis, 0, 0, tiled=True)  15 us
  transfers between devices with their start and end apart: 14, of which 6 were waited for; matrix products, arithmetic and copies ran while one was open for 12% of the time, Pallas kernels for 0%

profile of v3, /device:TPU:8, one launch (start us, length us, event | category | flops | bytes accessed | tf_op | source)
XLA Modules:
  0.0 264.0 jit_solution(13404090175007595146)
XLA Ops:
  7.2 0.0 all-gather.6.cloned.1.call-start
  7.2 1.6 constant_dynamic-slice_fusion.1
  8.8 0.0 all-gather.6.cloned.1.call-update
  8.8 0.0 all-gather.4.cloned.1.call-start
  8.9 1.9 slice.50
  10.8 0.0 all-gather.4.cloned.1.call-update
  10.8 24.3 %all-gather = s32[16,2080,2]{1,2,0:T(2,128)S(1)} all-gather(s32[1,2080,2]{1,2,0:T(2,128)} %bitcast.56), channel_id=1, replica_groups=mesh['x'=4,'y'=8,'z'=8,'c'=2] {'z','c'}, dimensions={0}, use_global_device_ids=true | all-gather | bytes 282880 | tf_op jit(solution)/shard_map/all_gather | solution.py:188
  35.1 0.3 reshape.127
  35.5 0.3 reshape.109
  35.8 0.2 reshape.110
  36.0 0.1 reshape.111
  36.1 0.1 dynamic-slice_reduce_fusion
  36.3 0.2 dynamic-slice_reduce_fusion.1
  36.5 0.1 dynamic-slice_reduce_fusion.5
  36.7 21.8 %all-gather.6.cloned.1.call-done.refs_1_ = bf16[4096,256]{1,0:T(8,128)(2,1)} async-done(((bf16[256,256]{1,0:T(8,128)(2,1)}), bf16[4096,256]{1,0:T(8,128)(2,1)}) %all-gather.6.cloned.1.call-update) | async-done | bytes 2097168 | tf_op jit(solution)/shard_map/all_gather | solution.py:179
  58.5 1.3 constant_dynamic-slice_fusion
  59.8 3.5 %collective-permute-start = (bf16[2048,256]{1,0:T(8,128)(2,1)S(1)}, bf16[2048,256]{1,0:T(8,128)(2,1)S(1)}, u32[]{:S(2)}, u32[]{:S(2)}) collective-permute-start(bf16[2048,256]{1,0:T(8,128)(2,1)S(1)} %constant_dynamic-slice_fusion), channel_id=1, source_target_pairs={{0,128},{128,256},{256,384},{384,0},{1,129},{129,257},{257,385},{3... | collective-permute-start | bytes 3145736 | tf_op jit(solution)/shard_map/ppermute | solution.py:183
  63.3 3.5 %collective-permute-start.1 = (bf16[2048,256]{1,0:T(8,128)(2,1)S(1)}, bf16[2048,256]{1,0:T(8,128)(2,1)S(1)}, u32[]{:S(2)}, u32[]{:S(2)}) collective-permute-start(bf16[2048,256]{1,0:T(8,128)(2,1)S(1)} %constant_dynamic-slice_fusion), channel_id=1, source_target_pairs={{0,384},{128,0},{256,128},{384,256},{1,385},{129,1},{257,129},{385... | collective-permute-start | bytes 3145736 | tf_op jit(solution)/shard_map/ppermute | solution.py:183
  67.0 1.2 slice_reduce_fusion.3
  68.2 20.0 %collective-permute-done.refs_2_ = bf16[2048,256]{1,0:T(8,128)(2,1)S(1)} collective-permute-done((bf16[2048,256]{1,0:T(8,128)(2,1)S(1)}, bf16[2048,256]{1,0:T(8,128)(2,1)S(1)}, u32[]{:S(2)}, u32[]{:S(2)}) %collective-permute-start) | collective-permute-done | bytes 1048608 | tf_op jit(solution)/shard_map/ppermute | solution.py:183
  88.2 2.3 collective-permute-start.2
  90.6 0.0 collective-permute-done.1.refs_3_
  90.6 0.0 copy-start.3
  90.6 4.7 %collective-permute-start.3 = (bf16[1024,256]{1,0:T(8,128)(2,1)S(1)}, bf16[1024,256]{1,0:T(8,128)(2,1)}, u32[]{:S(2)}, u32[]{:S(2)}) collective-permute-start(bf16[1024,256]{1,0:T(8,128)(2,1)S(1)} %slice.65), channel_id=1, source_target_pairs={{0,384},{128,0},{256,128},{384,256},{1,385},{129,1},{257,129},{385... | collective-permute-start | bytes 1572872 | tf_op jit(solution)/shard_map/ppermute | solution.py:184
  95.4 1.9 collective-permute-start.4
  97.3 2.4 collective-permute-start.5
  99.7 0.0 copy-start.4
  99.7 21.5 %fusion.hot_hbm = bf16[33280,128]{1,0:T(8,128)(2,1)} fusion(s32[128]{0:T(128)S(1)} %iota_and_fusion, s32[33280]{0:T(1024)S(1)} %get-tuple-element.3, s32[33280]{0:T(1024)S(1)} %get-tuple-element.2, pred[128]{0:T(512)(128)(4,1)S(1)} %iota_compare_fusion.2), kind=kLoop, calls=%fused_computation.1 | loop fusion | flops 17039360 | bytes 8786560 | tf_op jit(solution)/shard_map/convert_element_type | solution.py:226
  121.2 0.0 copy-done.2
  121.2 0.0 copy-done.3
  121.3 0.0 collective-permute-done.2.refs_4_
  121.3 1.9 collective-permute-start.6
  123.2 0.0 collective-permute-done.3.refs_5_
  123.2 2.6 collective-permute-start.7
  125.8 0.4 copy.31
  126.2 1.3 constant_dynamic-slice_fusion.2
  127.6 0.0 collective-permute-done.6.refs_8_
  127.6 0.0 collective-permute-done.7.refs_9_
  127.6 0.0 collective-permute-done.4.refs_6_
  127.6 0.0 collective-permute-done.5.refs_7_
  127.6 0.0 all-gather.4.cloned.1.call-done.refs_0_
  127.6 35.3 %chain.1 = bf16[8,64,256]{2,1,0:T(8,128)(2,1)} custom-call(f32[8,256]{1,0:T(8,128)} %get-tuple-element.21.state_ref, f32[8,256]{1,0:T(8,128)} %get-tuple-element.20.target_ref, s32[1,33280]{1,0:T(1,128)} %get-tuple-element.17.left_ref, s32[1,33280]{1,0:T(1,128)} %get-tuple-element.16.right_ref, bf16[33280,128]{1,0:T(8,128)(2,1)} %fusion.hot_hbm, ...), custom_call_target="tpu_custom_call" | custom-call | tf_op jit(solution)/shard_map/chain/pallas_call | solution.py:118
  163.0 4.2 %all-to-all-start = ((bf16[8,64,256]{2,1,0:T(8,128)(2,1)}), bf16[8,64,256]{2,1,0:T(8,128)(2,1)S(1)}, u32[]{:S(2)}, u32[]{:S(2)}) async-start(bf16[8,64,256]{2,1,0:T(8,128)(2,1)} %chain.1), calls=%async_computation | async-start | bytes 524288 | tf_op jit(solution)/shard_map/all_to_all | solution.py:203
  167.2 1.2 fusion.1
  168.4 11.1 %all-to-all-done.mine_ref = bf16[8,64,256]{2,1,0:T(8,128)(2,1)S(1)} async-done(((bf16[8,64,256]{2,1,0:T(8,128)(2,1)}), bf16[8,64,256]{2,1,0:T(8,128)(2,1)S(1)}, u32[]{:S(2)}, u32[]{:S(2)}) %all-to-all-start) | async-done | bytes 262176 | tf_op jit(solution)/shard_map/all_to_all | solution.py:203
  179.4 2.1 collective-permute-start.8
  181.6 0.9 select_bitcast_fusion.1
  182.5 0.4 collective-permute-done.8.other_ref
  182.9 2.0 grad.1
  184.9 0.0 copy-done
  184.9 0.0 copy-start.1
  184.9 19.7 %all_to_all.25 = bf16[4,576,256]{2,1,0:T(8,128)(2,1)S(1)} all-to-all(bf16[4,576,256]{2,1,0:T(8,128)(2,1)S(1)} %bitcast.51), channel_id=1, replica_groups=mesh['x'=4,'y'=8,'z'=8,'c'=2] {'x'}, dimensions={0} | all-to-all | bytes 2359296 | tf_op jit(solution)/shard_map/all_to_all | solution.py:203
  204.7 0.9 reduce_sum.21
  205.6 7.3 %all-to-all-start.2 = ((bf16[8,72,256]{2,1,0:T(8,128)(2,1)}), bf16[8,72,256]{2,1,0:T(8,128)(2,1)S(1)}, u32[]{:S(2)}, u32[]{:S(2)}) async-start(bf16[8,72,256]{2,1,0:T(8,128)(2,1)} %bitcast.11), calls=%async_computation.2 | async-start | bytes 589824 | tf_op jit(solution)/shard_map/all_to_all | solution.py:203
  212.9 10.7 %all-to-all-done.2 = bf16[8,72,256]{2,1,0:T(8,128)(2,1)S(1)} async-done(((bf16[8,72,256]{2,1,0:T(8,128)(2,1)}), bf16[8,72,256]{2,1,0:T(8,128)(2,1)S(1)}, u32[]{:S(2)}, u32[]{:S(2)}) %all-to-all-start.2) | async-done | bytes 294944 | tf_op jit(solution)/shard_map/all_to_all | solution.py:203
  223.6 0.0 copy-done.1
  223.6 0.9 multiply_convert_fusion
  224.6 13.3 %all_to_all.26 = bf16[8,72,256]{2,1,0:T(8,128)(2,1)S(1)} all-to-all(bf16[8,72,256]{2,1,0:T(8,128)(2,1)S(1)} %broadcast_in_dim.49), channel_id=1, replica_groups=mesh['x'=4,'y'=8,'z'=8,'c'=2] {'y'}, dimensions={0} | all-to-all | bytes 589824 | tf_op jit(solution)/shard_map/all_to_all | solution.py:203
  237.9 1.1 broadcast_in_dim.51
  239.0 3.5 %all-to-all-start.4 = ((bf16[4,576,256]{2,1,0:T(8,128)(2,1)}), bf16[4,576,256]{2,1,0:T(8,128)(2,1)S(1)}, u32[]{:S(2)}, u32[]{:S(2)}) async-start(bf16[4,576,256]{2,1,0:T(8,128)(2,1)} %broadcast_in_dim.51), calls=%async_computation.4 | async-start | bytes 2359296 | tf_op jit(solution)/shard_map/all_to_all | solution.py:203
  242.5 0.8 fusion.3
  243.3 0.7 copy.28
  244.0 12.1 %all-to-all-done.4 = bf16[4,576,256]{2,1,0:T(8,128)(2,1)S(1)} async-done(((bf16[4,576,256]{2,1,0:T(8,128)(2,1)}), bf16[4,576,256]{2,1,0:T(8,128)(2,1)S(1)}, u32[]{:S(2)}, u32[]{:S(2)}) %all-to-all-start.4) | async-done | bytes 1179680 | tf_op jit(solution)/shard_map/all_to_all | solution.py:203
  256.1 1.0 slice.70
  (35 shorter events, 0.5 us)
Async XLA Ops:
  7.2 51.3 %all-gather.6.cloned.1.call-start = ((), (), s32[]{:S(2)}) async-start(), calls=%async_computation.6 | async-start | bytes 2228224 | tf_op jit(solution)/shard_map/all_gather | solution.py:179
  8.8 118.8 %all-gather.4.cloned.1.call-start = ((), (), s32[]{:S(2)}) async-start(), calls=%async_computation.5 | async-start | bytes 9191424 | tf_op jit(solution)/shard_map/all_gather | solution.py:180
  59.8 28.4 %collective-permute-start = (bf16[2048,256]{1,0:T(8,128)(2,1)S(1)}, bf16[2048,256]{1,0:T(8,128)(2,1)S(1)}, u32[]{:S(2)}, u32[]{:S(2)}) collective-permute-start(bf16[2048,256]{1,0:T(8,128)(2,1)S(1)} %constant_dynamic-slice_fusion), channel_id=1, source_target_pairs={{0,128},{128,256},{256,384},{384,0},{1,129},{129,257},{257,385},{3... | collective-permute-start | bytes 3145736 | tf_op jit(solution)/shard_map/ppermute | solution.py:183
  63.3 27.3 %collective-permute-start.1 = (bf16[2048,256]{1,0:T(8,128)(2,1)S(1)}, bf16[2048,256]{1,0:T(8,128)(2,1)S(1)}, u32[]{:S(2)}, u32[]{:S(2)}) collective-permute-start(bf16[2048,256]{1,0:T(8,128)(2,1)S(1)} %constant_dynamic-slice_fusion), channel_id=1, source_target_pairs={{0,384},{128,0},{256,128},{384,256},{1,385},{129,1},{257,129},{385... | collective-permute-start | bytes 3145736 | tf_op jit(solution)/shard_map/ppermute | solution.py:183
  88.2 33.0 %copy-start.2 = (bf16[2048,256]{1,0:T(8,128)(2,1)}, bf16[2048,256]{1,0:T(8,128)(2,1)S(1)}, u32[]{:S(2)}) copy-start(bf16[2048,256]{1,0:T(8,128)(2,1)S(1)} %collective-permute-done.refs_2_) | copy-start | bytes 3145732
  88.2 33.0 %collective-permute-start.2 = (bf16[1024,256]{1,0:T(8,128)(2,1)S(1)}, bf16[1024,256]{1,0:T(8,128)(2,1)}, u32[]{:S(2)}, u32[]{:S(2)}) collective-permute-start(bf16[1024,256]{1,0:T(8,128)(2,1)S(1)} %slice.64), channel_id=1, source_target_pairs={{0,128},{128,256},{256,384},{384,0},{1,129},{129,257},{257,385},{3... | collective-permute-start | bytes 1572872 | tf_op jit(solution)/shard_map/ppermute | solution.py:184
  90.6 30.7 %copy-start.3 = (bf16[2048,256]{1,0:T(8,128)(2,1)}, bf16[2048,256]{1,0:T(8,128)(2,1)S(1)}, u32[]{:S(2)}) copy-start(bf16[2048,256]{1,0:T(8,128)(2,1)S(1)} %collective-permute-done.1.refs_3_) | copy-start | bytes 3145732
  90.6 32.6 %collective-permute-start.3 = (bf16[1024,256]{1,0:T(8,128)(2,1)S(1)}, bf16[1024,256]{1,0:T(8,128)(2,1)}, u32[]{:S(2)}, u32[]{:S(2)}) collective-permute-start(bf16[1024,256]{1,0:T(8,128)(2,1)S(1)} %slice.65), channel_id=1, source_target_pairs={{0,384},{128,0},{256,128},{384,256},{1,385},{129,1},{257,129},{385... | collective-permute-start | bytes 1572872 | tf_op jit(solution)/shard_map/ppermute | solution.py:184
  95.4 32.2 %collective-permute-start.4 = (bf16[2048,256]{1,0:T(8,128)(2,1)S(1)}, bf16[2048,256]{1,0:T(8,128)(2,1)}, u32[]{:S(2)}, u32[]{:S(2)}) collective-permute-start(bf16[2048,256]{1,0:T(8,128)(2,1)S(1)} %collective-permute-done.refs_2_), channel_id=1, source_target_pairs={{0,1},{1,0},{2,3},{3,2},{4,5},{5,4},{6,7},{7,6},{8,9},{9,8},{10,11... | collective-permute-start | bytes 3145736 | tf_op jit(solution)/shard_map/ppermute | solution.py:186
  97.3 30.3 %collective-permute-start.5 = (bf16[2048,256]{1,0:T(8,128)(2,1)S(1)}, bf16[2048,256]{1,0:T(8,128)(2,1)}, u32[]{:S(2)}, u32[]{:S(2)}) collective-permute-start(bf16[2048,256]{1,0:T(8,128)(2,1)S(1)} %collective-permute-done.1.refs_3_), channel_id=1, source_target_pairs={{0,1},{1,0},{2,3},{3,2},{4,5},{5,4},{6,7},{7,6},{8,9},{9,8},{10,11... | collective-permute-start | bytes 3145736 | tf_op jit(solution)/shard_map/ppermute | solution.py:186
  99.7 26.1 %copy-start.4 = (s32[2,2080]{1,0:T(2,128)S(1)}, s32[2,2080]{1,0:T(2,128)}, u32[]{:S(2)}) copy-start(s32[2,2080]{1,0:T(2,128)} %param.8) | copy-start | bytes 49924
  121.3 6.3 %collective-permute-start.6 = (bf16[1024,256]{1,0:T(8,128)(2,1)}, bf16[1024,256]{1,0:T(8,128)(2,1)}, u32[]{:S(2)}, u32[]{:S(2)}) collective-permute-start(bf16[1024,256]{1,0:T(8,128)(2,1)} %collective-permute-done.2.refs_4_), channel_id=1, source_target_pairs={{0,1},{1,0},{2,3},{3,2},{4,5},{5,4},{6,7},{7,6},{8,9},{9,8},{10,11... | collective-permute-start | bytes 1572872 | tf_op jit(solution)/shard_map/ppermute | solution.py:186
  123.2 4.4 %collective-permute-start.7 = (bf16[1024,256]{1,0:T(8,128)(2,1)}, bf16[1024,256]{1,0:T(8,128)(2,1)}, u32[]{:S(2)}, u32[]{:S(2)}) collective-permute-start(bf16[1024,256]{1,0:T(8,128)(2,1)} %collective-permute-done.3.refs_5_), channel_id=1, source_target_pairs={{0,1},{1,0},{2,3},{3,2},{4,5},{5,4},{6,7},{7,6},{8,9},{9,8},{10,11... | collective-permute-start | bytes 1572872 | tf_op jit(solution)/shard_map/ppermute | solution.py:186
  163.0 16.4 %all-to-all-start = ((bf16[8,64,256]{2,1,0:T(8,128)(2,1)}), bf16[8,64,256]{2,1,0:T(8,128)(2,1)S(1)}, u32[]{:S(2)}, u32[]{:S(2)}) async-start(bf16[8,64,256]{2,1,0:T(8,128)(2,1)} %chain.1), calls=%async_computation | async-start | bytes 524288 | tf_op jit(solution)/shard_map/all_to_all | solution.py:203
  179.4 3.4 %collective-permute-start.8 = (bf16[8,64,256]{2,1,0:T(8,128)(2,1)S(1)}, bf16[8,64,256]{2,1,0:T(8,128)(2,1)S(1)}, u32[]{:S(2)}, u32[]{:S(2)}) collective-permute-start(bf16[8,64,256]{2,1,0:T(8,128)(2,1)S(1)} %all-to-all-done.mine_ref), channel_id=1, source_target_pairs={{0,1},{1,0},{2,3},{3,2},{4,5},{5,4},{6,7},{7,6},{8,9},{9,8},{10,11... | collective-permute-start | bytes 786440 | tf_op jit(solution)/shard_map/ppermute | solution.py:243
  182.8 2.0 copy-start
  184.9 38.7 %copy-start.1 = (bf16[2080,256]{1,0:T(8,128)(2,1)S(1)}, bf16[2080,256]{1,0:T(8,128)(2,1)}, u32[]{:S(2)}) copy-start(bf16[2080,256]{1,0:T(8,128)(2,1)} %param.7) | copy-start | bytes 3194884
  205.6 18.0 %all-to-all-start.2 = ((bf16[8,72,256]{2,1,0:T(8,128)(2,1)}), bf16[8,72,256]{2,1,0:T(8,128)(2,1)S(1)}, u32[]{:S(2)}, u32[]{:S(2)}) async-start(bf16[8,72,256]{2,1,0:T(8,128)(2,1)} %bitcast.11), calls=%async_computation.2 | async-start | bytes 589824 | tf_op jit(solution)/shard_map/all_to_all | solution.py:203
  239.0 17.1 %all-to-all-start.4 = ((bf16[4,576,256]{2,1,0:T(8,128)(2,1)}), bf16[4,576,256]{2,1,0:T(8,128)(2,1)S(1)}, u32[]{:S(2)}, u32[]{:S(2)}) async-start(bf16[4,576,256]{2,1,0:T(8,128)(2,1)} %broadcast_in_dim.51), calls=%async_computation.4 | async-start | bytes 2359296 | tf_op jit(solution)/shard_map/all_to_all | solution.py:203
Sparse Core Ops, SparseCore 0:
  10.7 47.7 all-gather.5
  60.6 58.6 all-gather.3

commit v4 on v3

--- a/solution.py
+++ b/solution.py
@@ -12,7 +12,7 @@
 NT = (((1,), (1,)), ((), ()))
 CHUNK = 1664
 FETCH = 2048
-PIECE = 256
+PIECE = 64
 AXES = ("x", "y", "z", "c")
 FULL = pl.BlockSpec(memory_space=pltpu.VMEM)
 
@@ -34,7 +34,6 @@
     for copy in fetches:
         copy.start()
     hot_copy = pltpu.make_async_copy(hot_hbm, hot_ref, sems.at[len(fetches)])
-    hot_copy.start()
     state = state_ref[...]
 
     def derive(y, s, waits=None):
@@ -82,6 +81,7 @@
         return jnp.concatenate(left, 1) + jnp.concatenate(right, 1)
 
     k1 = derive(state, 0, list(fetches))
+    hot_copy.start()
     keep_ref[0] = state
     keep_ref[1] = state + 0.5 * DT * k1
 
@@ -152,15 +152,13 @@
         theta = (zl * zr).astype(jnp.bfloat16)
         grad = scale * jnp.dot(theta, g, preferred_element_type=jnp.float32)
         out_ref[at, :] = grad.astype(jnp.bfloat16)
-    rest = out_ref.shape[0] - cands
-    out_ref[cands:, :] = jnp.zeros((rest, modes), jnp.bfloat16)
-
-
-def run_grad(first, mine, other, left, right, consts, total, height):
+
+
+def run_grad(first, mine, other, left, right, consts, total):
     modes = mine.shape[2]
     return pl.pallas_call(
         functools.partial(grad_kernel, 1.0 / math.sqrt(total), 416),
-        out_shape=jax.ShapeDtypeStruct((height, modes), jnp.bfloat16),
+        out_shape=jax.ShapeDtypeStruct((left.shape[0], modes), jnp.bfloat16),
         in_specs=[FULL] * 6,
         out_specs=FULL,
         compiler_params=pltpu.CompilerParams(vmem_limit_bytes=32 * 2**20),
@@ -168,45 +166,31 @@
     )(first, mine, other, left, right, consts)
 
 
-def gather_candidates(coeffs, pairs):
-    nx, nz, nc = [lax.axis_size(axis) for axis in ("x", "z", "c")]
-    cands, side = nz * nc, PIECE * nx
-    x, core = lax.axis_index("x"), lax.axis_index("c")
-    ahead = [(i, (i + 1) % nx) for i in range(nx)]
-    behind = [(i, (i - 1) % nx) for i in range(nx)]
-    swap = [(0, 1), (1, 0)]
-
-    mine = lax.all_gather(lax.dynamic_slice_in_dim(coeffs, x * PIECE, PIECE, 0), ("z", "c"), axis=0, tiled=True)
-    rest = lax.all_gather(coeffs[side:], ("z", "c"), axis=0, tiled=True)
-    half = mine.shape[0] // 2
-    part = lax.dynamic_slice_in_dim(mine, core * half, half, 0)
-    one, three = lax.ppermute(part, "x", ahead), lax.ppermute(part, "x", behind)
-    two = [lax.ppermute(one[: half // 2], "x", ahead), lax.ppermute(three[half // 2 :], "x", behind)]
-    got = [one, three, *two]
-    blocks = [rest, mine, *got, *[lax.ppermute(block, "c", swap) for block in got]]
-
-    index = lax.all_gather(pairs, ("z", "c"), axis=1, tiled=True).reshape(2, cands, -1)
-    sides = index[:, :, :side].reshape(2, cands, nx, PIECE)
-
-    def piece(away, first, count):
-        which = lax.rem(x + away, nx)
-        return lax.dynamic_slice(sides, (0, first, which, 0), (2, count, 1, PIECE)).reshape(2, count * PIECE)
-
-    order = [index[:, :, side:].reshape(2, -1), piece(0, 0, cands)]
-    for first in (core * (cands // 2), (1 - core) * (cands // 2)):
-        order += [piece(nx - 1, first, cands // 2), piece(1, first, cands // 2)]
-        order += [piece(2, first, cands // 4), piece(2, first + cands // 4, cands // 4)]
-    return blocks, jnp.concatenate(order, 1)
-
-
 def exchange(blocks, axis):
     return lax.all_to_all(blocks, axis, 0, 0, tiled=True)
 
 
-def spread(block, axis):
-    count = lax.axis_size(axis)
+def spread(block, axis, count):
     blocks = exchange(jnp.broadcast_to(block[None], (count, *block.shape)), axis)
     return blocks.reshape(count * block.shape[0], *block.shape[1:])
+
+
+def gather_candidates(coeffs, pairs):
+    ny, nz, nc = [lax.axis_size(axis) for axis in ("y", "z", "c")]
+    side = PIECE * ny
+    core = lax.axis_index("c")
+    piece = lax.dynamic_slice_in_dim(coeffs, lax.axis_index("y") * PIECE, PIECE, 0)
+    rest = lax.all_gather(coeffs[side:], ("z", "c"), axis=0, tiled=True)
+    mine = spread(spread(piece, "z", nz), "y", ny)
+    other = lax.ppermute(mine, "c", [(0, 1), (1, 0)])
+
+    index = spread(pairs[None], ("z", "c"), nz * nc).reshape(nz, nc, 2, -1).transpose(2, 0, 1, 3)
+    order = [index[..., side:].reshape(2, -1)]
+    sides = index[..., :side].reshape(2, nz, nc, ny, PIECE)
+    for which in (core, 1 - core):
+        part = jnp.where(which == 0, sides[:, :, 0], sides[:, :, 1])
+        order.append(part.transpose(0, 2, 1, 3).reshape(2, -1))
+    return [rest, mine, other], jnp.concatenate(order, 1)
 
 
 def body(state, target, coeffs, pairs, mask):
@@ -231,30 +215,31 @@
     by_core = state.reshape(nz, nc, rows, modes)
     first = jnp.where(core == 0, by_core[:, 0], by_core[:, 1]), jnp.where(core == 0, by_core[:, 1], by_core[:, 0])
     first = jnp.stack(first)
-    piece = -(-own // (8 * nx * ny)) * 8
-    height = piece * nx * ny
-    at = lax.axis_index(("x", "y")) * piece
-    fill = ((0, height - own), (0, 0))
+    quarter = own // nx
+    piece = -(-quarter // (8 * ny)) * 8
+    extra = piece * ny - quarter
+    at = lax.axis_index("x") * quarter + lax.axis_index("y") * piece
+    fill = ((0, extra), (0, 0))
     coeffs_piece = lax.dynamic_slice_in_dim(jnp.pad(coeffs, fill), at, piece, 0).astype(jnp.float32)
     mask_piece = lax.dynamic_slice_in_dim(jnp.pad(mask, fill), at, piece, 0).astype(jnp.float32)
 
     packed = run_chain(state_own, target_own, index[0:1], index[1:2], hot, blocks, nz, segments)
     mine = exchange(packed, "z")
     other = lax.ppermute(mine, "c", [(0, 1), (1, 0)])
-    grad = run_grad(first, mine, other, left_hot, right_hot, consts, total, height)
+    grad = run_grad(first, mine, other, left_hot, right_hot, consts, total)
 
     slopes = [block[:, :rows].astype(jnp.float32) for block in (mine, other)]
     slope = jnp.stack([jnp.where(core == 0, *slopes), jnp.where(core == 0, *slopes[::-1])], 1)
     slope = slope.reshape(block_rows, modes)
 
-    grad = exchange(grad.reshape(nx, ny * piece, modes), "x")
-    grad = jnp.sum(grad.astype(jnp.float32), axis=0).astype(jnp.bfloat16)
+    grad = exchange(grad.reshape(nx, quarter, modes), "x")
+    grad = jnp.pad(jnp.sum(grad.astype(jnp.float32), axis=0).astype(jnp.bfloat16), fill)
     grad = exchange(grad.reshape(ny, piece, modes), "y")
     grad = jnp.sum(grad.astype(jnp.float32), axis=0)
     rate = 0.5 * math.sqrt(segments * total) / DT
     fresh = (mask_piece * (coeffs_piece - rate * grad)).astype(jnp.bfloat16)
-    fresh = spread(spread(fresh, "y"), "x")
-    return slope, fresh[:own]
+    fresh = spread(spread(fresh, "y", ny)[:quarter], "x", nx)
+    return slope, fresh
 
 
 def solution(mesh):

time: 265 us -> 264 us (level)
  waiting for transfers between devices: 76.1 us -> 92 us
  starting transfers between devices: 40.1 us -> 27.1 us
  other arithmetic: 26.3 us -> 22.6 us
    all_to_all x3 -> x5, waiting for transfers between devices: 33.9 us -> 91.3 us  [exchange(): return lax.all_to_all(blocks, axis, 0, 0, tiled=True)]
    all_gather x1 -> x0, blocking collectives: 24.3 us -> none  [gather_candidates(): lax.all_gather(pairs, ('z', 'c'), axis=1, tiled=True).reshape(2, cands, -1)]
    all_to_all x2 -> x3, blocking collectives: 33.1 us -> 55.2 us  [exchange(): return lax.all_to_all(blocks, axis, 0, 0, tiled=True)]
    all_gather x1 -> x0, waiting for transfers between devices: 21.8 us -> none  [gather_candidates(): lax.all_gather(lax.dynamic_slice_in_dim(coeffs, x * PIECE, PIECE, 0), ('z...]
    ppermute x8 -> x1, starting transfers between devices: 22.9 us -> 2.09 us  [gather_candidates(): other = lax.ppermute(mine, 'c', [(0, 1), (1, 0)])]
    ppermute x8 -> x1, waiting for transfers between devices: 20 us -> 0.01 us  [gather_candidates(): other = lax.ppermute(mine, 'c', [(0, 1), (1, 0)])]
    all_to_all x3 -> x5, starting transfers between devices: 15 us -> 23 us  [exchange(): return lax.all_to_all(blocks, axis, 0, 0, tiled=True)]
    convert_element_type x1, other arithmetic: 21.5 us -> 18.4 us  [body(): hot = (low == lane & 63).astype(jnp.bfloat16)]
  transfers between devices with their start and end apart: 14 -> 8, of which waited for: 6 -> 6; matrix products, arithmetic and copies ran while one was open for 12% -> 12% of each run, Pallas kernels for 0% -> 0%
where the time goes in v4:
time: 264 us; the launch traced here: 263 us
  waiting for transfers between devices  92 us (35%)
  blocking collectives  55.2 us (21%)
  Pallas kernels  37.4 us (14%)
  starting transfers between devices  27.1 us (10%)
  other arithmetic  22.6 us (9%)
  local copies, waits for them, and re-layouts  14.5 us (5%)
  between operations  14.3 us (5%)
    all_to_all x5, waiting for transfers between devices, exchange(): return lax.all_to_all(blocks, axis, 0, 0, tiled=True)  91.3 us
    all_to_all x3, blocking collectives, exchange(): return lax.all_to_all(blocks, axis, 0, 0, tiled=True)  55.2 us
    pallas_call x1, Pallas kernels, run_chain(): pl.pallas_call(functools.partial(chain_kernel, 1.0 / math.sqrt(total), se...  35.3 us
    all_to_all x5, starting transfers between devices, exchange(): return lax.all_to_all(blocks, axis, 0, 0, tiled=True)  23 us
    convert_element_type x1, other arithmetic, body(): hot = (low == lane & 63).astype(jnp.bfloat16)  18.4 us
  transfers between devices with their start and end apart: 8, of which 6 were waited for; matrix products, arithmetic and copies ran while one was open for 12% of the time, Pallas kernels for 0%

profile of v4, /device:TPU:8, one launch (start us, length us, event | category | flops | bytes accessed | tf_op | source)
XLA Modules:
  0.0 263.0 jit_solution(764282289337338713)
XLA Ops:
  7.2 0.0 copy-start.3
  7.2 0.0 all-gather.2.cloned.1.call-start
  7.2 2.1 slice.54
  9.3 0.0 all-gather.2.cloned.1.call-update
  9.3 0.8 constant_dynamic-slice_fusion
  10.1 22.0 %all_to_all.40 = bf16[8,64,256]{2,1,0:T(8,128)(2,1)S(1)} all-to-all(bf16[8,64,256]{2,1,0:T(8,128)(2,1)S(1)} %broadcast_in_dim.67), channel_id=1, replica_groups=mesh['x'=4,'y'=8,'z'=8,'c'=2] {'z'}, dimensions={0} | all-to-all | bytes 524288 | tf_op jit(solution)/shard_map/all_to_all | solution.py:170
  32.1 0.0 copy-done.3
  32.1 0.8 broadcast_in_dim.61
  32.9 3.5 %all-to-all-start = ((s32[16,1,2,2080]{3,2,1,0:T(2,128)}), s32[16,1,2,2080]{3,2,1,0:T(2,128)S(1)}, u32[]{:S(2)}, u32[]{:S(2)}) async-start(s32[16,1,2,2080]{3,2,1,0:T(2,128)} %broadcast_in_dim.61), calls=%async_computation | async-start | bytes 557056 | tf_op jit(solution)/shard_map/all_to_all | solution.py:170
  36.5 0.4 copy.51
  36.9 1.3 constant_dynamic-slice_fusion.1
  38.2 13.0 %all-to-all-done = s32[16,1,2,2080]{3,2,1,0:T(2,128)S(1)} async-done(((s32[16,1,2,2080]{3,2,1,0:T(2,128)}), s32[16,1,2,2080]{3,2,1,0:T(2,128)S(1)}, u32[]{:S(2)}, u32[]{:S(2)}) %all-to-all-start) | async-done | bytes 266272 | tf_op jit(solution)/shard_map/all_to_all | solution.py:170
  51.2 1.4 broadcast_in_dim.69
  52.6 7.5 %all-to-all-start.2 = ((bf16[8,512,256]{2,1,0:T(8,128)(2,1)}), bf16[8,512,256]{2,1,0:T(8,128)(2,1)S(1)}, u32[]{:S(2)}, u32[]{:S(2)}) async-start(bf16[8,512,256]{2,1,0:T(8,128)(2,1)} %broadcast_in_dim.69), calls=%async_computation.2 | async-start | bytes 4194304 | tf_op jit(solution)/shard_map/all_to_all | solution.py:170
  60.2 0.1 copy.44
  60.3 1.0 reshape.100
  61.4 0.1 reshape.101
  61.5 0.1 reshape.102
  61.6 0.1 reshape.103
  61.7 1.0 constant_dynamic-update-slice_fusion.2
  62.8 1.7 slice_reduce_fusion.3
  64.5 46.2 %all-to-all-done.2 = bf16[8,512,256]{2,1,0:T(8,128)(2,1)S(1)} async-done(((bf16[8,512,256]{2,1,0:T(8,128)(2,1)}), bf16[8,512,256]{2,1,0:T(8,128)(2,1)S(1)}, u32[]{:S(2)}, u32[]{:S(2)}) %all-to-all-start.2) | async-done | bytes 2097184 | tf_op jit(solution)/shard_map/all_to_all | solution.py:170
  110.7 0.0 copy-start.1
  110.7 2.1 collective-permute-start
  112.8 18.4 %fusion.hot_hbm = bf16[33280,128]{1,0:T(8,128)(2,1)} fusion(s32[128]{0:T(128)S(1)} %iota_and_fusion, s32[33280]{0:T(1024)} %get-tuple-element.3, s32[33280]{0:T(1024)} %get-tuple-element.2, pred[128]{0:T(512)(128)(4,1)S(1)} %iota_compare_fusion.2), kind=kLoop, calls=%fused_computation.1 | loop fusion | flops 17039360 | bytes 8786560 | tf_op jit(solution)/shard_map/convert_element_type | solution.py:210
  131.2 0.0 copy-done.1
  131.2 0.0 collective-permute-done.refs_2_
  131.2 0.0 all-gather.2.cloned.1.call-done.refs_0_
  131.2 35.3 %chain.1 = bf16[8,64,256]{2,1,0:T(8,128)(2,1)} custom-call(f32[8,256]{1,0:T(8,128)} %get-tuple-element.15.state_ref, f32[8,256]{1,0:T(8,128)} %get-tuple-element.14.target_ref, s32[1,33280]{1,0:T(1,128)} %get-tuple-element.9.left_ref, s32[1,33280]{1,0:T(1,128)} %get-tuple-element.8.right_ref, bf16[33280,128]{1,0:T(8,128)(2,1)} %fusion.hot_hbm, ...), custom_call_target="tpu_custom_call" | custom-call | tf_op jit(solution)/shard_map/chain/pallas_call | solution.py:118
  166.6 3.6 %all-to-all-start.3 = ((bf16[8,64,256]{2,1,0:T(8,128)(2,1)}), bf16[8,64,256]{2,1,0:T(8,128)(2,1)S(1)}, u32[]{:S(2)}, u32[]{:S(2)}) async-start(bf16[8,64,256]{2,1,0:T(8,128)(2,1)} %chain.1), calls=%async_computation.3 | async-start | bytes 524288 | tf_op jit(solution)/shard_map/all_to_all | solution.py:170
  170.2 1.2 fusion.1
  171.5 10.7 %all-to-all-done.3.mine_ref = bf16[8,64,256]{2,1,0:T(8,128)(2,1)S(1)} async-done(((bf16[8,64,256]{2,1,0:T(8,128)(2,1)}), bf16[8,64,256]{2,1,0:T(8,128)(2,1)S(1)}, u32[]{:S(2)}, u32[]{:S(2)}) %all-to-all-start.3) | async-done | bytes 262176 | tf_op jit(solution)/shard_map/all_to_all | solution.py:170
  182.2 1.9 collective-permute-start.1
  184.1 0.9 select_bitcast_fusion.1
  185.0 0.6 collective-permute-done.1.other_ref
  185.6 0.0 copy-start
  185.6 2.0 grad.1
  187.6 0.0 copy-done
  187.6 0.0 copy-start.2
  187.7 19.8 %all_to_all.41 = bf16[4,520,256]{2,1,0:T(8,128)(2,1)S(1)} all-to-all(bf16[4,520,256]{2,1,0:T(8,128)(2,1)S(1)} %bitcast.49), channel_id=1, replica_groups=mesh['x'=4,'y'=8,'z'=8,'c'=2] {'x'}, dimensions={0} | all-to-all | bytes 2129920 | tf_op jit(solution)/shard_map/all_to_all | solution.py:170
  207.4 0.3 reduce_sum.21
  207.7 0.7 pad.14
  208.5 4.8 %all-to-all-start.5 = ((bf16[8,72,256]{2,1,0:T(8,128)(2,1)}), bf16[8,72,256]{2,1,0:T(8,128)(2,1)S(1)}, u32[]{:S(2)}, u32[]{:S(2)}) async-start(bf16[8,72,256]{2,1,0:T(8,128)(2,1)} %bitcast.17), calls=%async_computation.5 | async-start | bytes 589824 | tf_op jit(solution)/shard_map/all_to_all | solution.py:170
  213.2 10.6 %all-to-all-done.5 = bf16[8,72,256]{2,1,0:T(8,128)(2,1)S(1)} async-done(((bf16[8,72,256]{2,1,0:T(8,128)(2,1)}), bf16[8,72,256]{2,1,0:T(8,128)(2,1)S(1)}, u32[]{:S(2)}, u32[]{:S(2)}) %all-to-all-start.5) | async-done | bytes 294944 | tf_op jit(solution)/shard_map/all_to_all | solution.py:170
  223.9 0.0 copy-done.2
  223.9 0.9 multiply_convert_fusion
  224.8 13.4 %all_to_all.42 = bf16[8,72,256]{2,1,0:T(8,128)(2,1)S(1)} all-to-all(bf16[8,72,256]{2,1,0:T(8,128)(2,1)S(1)} %broadcast_in_dim.70), channel_id=1, replica_groups=mesh['x'=4,'y'=8,'z'=8,'c'=2] {'y'}, dimensions={0} | all-to-all | bytes 589824 | tf_op jit(solution)/shard_map/all_to_all | solution.py:170
  238.2 1.0 broadcast_in_dim.71
  239.3 3.5 %all-to-all-start.7 = ((bf16[4,520,256]{2,1,0:T(8,128)(2,1)}), bf16[4,520,256]{2,1,0:T(8,128)(2,1)S(1)}, u32[]{:S(2)}, u32[]{:S(2)}) async-start(bf16[4,520,256]{2,1,0:T(8,128)(2,1)} %broadcast_in_dim.71), calls=%async_computation.7 | async-start | bytes 2129920 | tf_op jit(solution)/shard_map/all_to_all | solution.py:170
  242.8 0.8 fusion.3
  243.6 0.7 copy.48
  244.3 10.9 %all-to-all-done.7 = bf16[4,520,256]{2,1,0:T(8,128)(2,1)S(1)} async-done(((bf16[4,520,256]{2,1,0:T(8,128)(2,1)}), bf16[4,520,256]{2,1,0:T(8,128)(2,1)S(1)}, u32[]{:S(2)}, u32[]{:S(2)}) %all-to-all-start.7) | async-done | bytes 1064992 | tf_op jit(solution)/shard_map/all_to_all | solution.py:170
  255.2 1.0 copy.57
  (18 shorter events, 0.3 us)
Async XLA Ops:
  7.2 24.9 %copy-start.3 = (s32[2,2080]{1,0:T(2,128)S(1)}, s32[2,2080]{1,0:T(2,128)}, u32[]{:S(2)}) copy-start(s32[2,2080]{1,0:T(2,128)} %param.8) | copy-start | bytes 49924
  7.2 124.0 %all-gather.2.cloned.1.call-start = ((), (), s32[]{:S(2)}) async-start(), calls=%async_computation.8 | async-start | bytes 13647872 | tf_op jit(solution)/shard_map/all_gather | solution.py:183
  32.9 18.3 %all-to-all-start = ((s32[16,1,2,2080]{3,2,1,0:T(2,128)}), s32[16,1,2,2080]{3,2,1,0:T(2,128)S(1)}, u32[]{:S(2)}, u32[]{:S(2)}) async-start(s32[16,1,2,2080]{3,2,1,0:T(2,128)} %broadcast_in_dim.61), calls=%async_computation | async-start | bytes 557056 | tf_op jit(solution)/shard_map/all_to_all | solution.py:170
  52.6 58.0 %all-to-all-start.2 = ((bf16[8,512,256]{2,1,0:T(8,128)(2,1)}), bf16[8,512,256]{2,1,0:T(8,128)(2,1)S(1)}, u32[]{:S(2)}, u32[]{:S(2)}) async-start(bf16[8,512,256]{2,1,0:T(8,128)(2,1)} %broadcast_in_dim.69), calls=%async_computation.2 | async-start | bytes 4194304 | tf_op jit(solution)/shard_map/all_to_all | solution.py:170
  110.7 20.5 %copy-start.1 = (bf16[8,512,256]{2,1,0:T(8,128)(2,1)}, bf16[8,512,256]{2,1,0:T(8,128)(2,1)S(1)}, u32[]{:S(2)}) copy-start(bf16[8,512,256]{2,1,0:T(8,128)(2,1)S(1)} %all-to-all-done.2) | copy-start | bytes 6291460
  110.7 20.5 %collective-permute-start = (bf16[4096,256]{1,0:T(8,128)(2,1)S(1)}, bf16[4096,256]{1,0:T(8,128)(2,1)}, u32[]{:S(2)}, u32[]{:S(2)}) collective-permute-start(bf16[4096,256]{1,0:T(8,128)(2,1)S(1)} %bitcast.50), channel_id=1, source_target_pairs={{0,1},{1,0},{2,3},{3,2},{4,5},{5,4},{6,7},{7,6},{8,9},{9,8},{10,11... | collective-permute-start | bytes 6291464 | tf_op jit(solution)/shard_map/ppermute | solution.py:185
  166.6 15.6 %all-to-all-start.3 = ((bf16[8,64,256]{2,1,0:T(8,128)(2,1)}), bf16[8,64,256]{2,1,0:T(8,128)(2,1)S(1)}, u32[]{:S(2)}, u32[]{:S(2)}) async-start(bf16[8,64,256]{2,1,0:T(8,128)(2,1)} %chain.1), calls=%async_computation.3 | async-start | bytes 524288 | tf_op jit(solution)/shard_map/all_to_all | solution.py:170
  182.2 3.4 %collective-permute-start.1 = (bf16[8,64,256]{2,1,0:T(8,128)(2,1)S(1)}, bf16[8,64,256]{2,1,0:T(8,128)(2,1)S(1)}, u32[]{:S(2)}, u32[]{:S(2)}) collective-permute-start(bf16[8,64,256]{2,1,0:T(8,128)(2,1)S(1)} %all-to-all-done.3.mine_ref), channel_id=1, source_target_pairs={{0,1},{1,0},{2,3},{3,2},{4,5},{5,4},{6,7},{7,6},{8,9},{9,8},{10,11... | collective-permute-start | bytes 786440 | tf_op jit(solution)/shard_map/ppermute | solution.py:228
  185.6 2.0 copy-start
  187.6 36.2 %copy-start.2 = (bf16[2080,256]{1,0:T(8,128)(2,1)S(1)}, bf16[2080,256]{1,0:T(8,128)(2,1)}, u32[]{:S(2)}) copy-start(bf16[2080,256]{1,0:T(8,128)(2,1)} %param.7) | copy-start | bytes 3194884
  208.5 15.4 %all-to-all-start.5 = ((bf16[8,72,256]{2,1,0:T(8,128)(2,1)}), bf16[8,72,256]{2,1,0:T(8,128)(2,1)S(1)}, u32[]{:S(2)}, u32[]{:S(2)}) async-start(bf16[8,72,256]{2,1,0:T(8,128)(2,1)} %bitcast.17), calls=%async_computation.5 | async-start | bytes 589824 | tf_op jit(solution)/shard_map/all_to_all | solution.py:170
  239.3 15.9 %all-to-all-start.7 = ((bf16[4,520,256]{2,1,0:T(8,128)(2,1)}), bf16[4,520,256]{2,1,0:T(8,128)(2,1)S(1)}, u32[]{:S(2)}, u32[]{:S(2)}) async-start(bf16[4,520,256]{2,1,0:T(8,128)(2,1)} %broadcast_in_dim.71), calls=%async_computation.7 | async-start | bytes 2129920 | tf_op jit(solution)/shard_map/all_to_all | solution.py:170
Sparse Core Ops, SparseCore 0:
  10.7 90.8 all-gather.1

commit v5 on v4

--- a/solution.py
+++ b/solution.py
@@ -12,7 +12,6 @@
 NT = (((1,), (1,)), ((), ()))
 CHUNK = 1664
 FETCH = 2048
-PIECE = 64
 AXES = ("x", "y", "z", "c")
 FULL = pl.BlockSpec(memory_space=pltpu.VMEM)
 
@@ -175,24 +174,6 @@
     return blocks.reshape(count * block.shape[0], *block.shape[1:])
 
 
-def gather_candidates(coeffs, pairs):
-    ny, nz, nc = [lax.axis_size(axis) for axis in ("y", "z", "c")]
-    side = PIECE * ny
-    core = lax.axis_index("c")
-    piece = lax.dynamic_slice_in_dim(coeffs, lax.axis_index("y") * PIECE, PIECE, 0)
-    rest = lax.all_gather(coeffs[side:], ("z", "c"), axis=0, tiled=True)
-    mine = spread(spread(piece, "z", nz), "y", ny)
-    other = lax.ppermute(mine, "c", [(0, 1), (1, 0)])
-
-    index = spread(pairs[None], ("z", "c"), nz * nc).reshape(nz, nc, 2, -1).transpose(2, 0, 1, 3)
-    order = [index[..., side:].reshape(2, -1)]
-    sides = index[..., :side].reshape(2, nz, nc, ny, PIECE)
-    for which in (core, 1 - core):
-        part = jnp.where(which == 0, sides[:, :, 0], sides[:, :, 1])
-        order.append(part.transpose(0, 2, 1, 3).reshape(2, -1))
-    return [rest, mine, other], jnp.concatenate(order, 1)
-
-
 def body(state, target, coeffs, pairs, mask):
     block_rows, modes = state.shape
     own = coeffs.shape[0]
@@ -202,7 +183,8 @@
     core = lax.axis_index("c")
     start = lax.axis_index(("z", "c")) * rows
 
-    blocks, index = gather_candidates(coeffs, pairs)
+    weights = lax.all_gather(coeffs, ("z", "c"), axis=0, tiled=True)
+    index = lax.all_gather(pairs, ("z", "c"), axis=1, tiled=True)
     state_own = lax.dynamic_slice_in_dim(state, start, rows, 0)
     target_own = lax.dynamic_slice_in_dim(target, start, rows, 0)
     lane = jnp.arange(128, dtype=jnp.int32)[None, :]
@@ -223,7 +205,7 @@
     coeffs_piece = lax.dynamic_slice_in_dim(jnp.pad(coeffs, fill), at, piece, 0).astype(jnp.float32)
     mask_piece = lax.dynamic_slice_in_dim(jnp.pad(mask, fill), at, piece, 0).astype(jnp.float32)
 
-    packed = run_chain(state_own, target_own, index[0:1], index[1:2], hot, blocks, nz, segments)
+    packed = run_chain(state_own, target_own, index[0:1], index[1:2], hot, [weights], nz, segments)
     mine = exchange(packed, "z")
     other = lax.ppermute(mine, "c", [(0, 1), (1, 0)])
     grad = run_grad(first, mine, other, left_hot, right_hot, consts, total)

time: 264 us -> 250 us (0.947)
  starting transfers between devices: 27.1 us -> 16.8 us
  local copies, waits for them, and re-layouts: 14.5 us -> 6.75 us
  other arithmetic: 22.6 us -> 25.6 us
    all_to_all x5 -> x3, waiting for transfers between devices: 91.3 us -> 32.2 us  [exchange(): return lax.all_to_all(blocks, axis, 0, 0, tiled=True)]
    all_gather x1, waiting for transfers between devices: 0.02 us -> 58 us  [body(): weights = lax.all_gather(coeffs, ('z', 'c'), axis=0, tiled=True)]
    all_gather x0 -> x1, blocking collectives: none -> 24.2 us  [body(): index = lax.all_gather(pairs, ('z', 'c'), axis=1, tiled=True)]
    all_to_all x3 -> x2, blocking collectives: 55.2 us -> 33 us  [exchange(): return lax.all_to_all(blocks, axis, 0, 0, tiled=True)]
    all_to_all x5 -> x3, starting transfers between devices: 23 us -> 14.8 us  [exchange(): return lax.all_to_all(blocks, axis, 0, 0, tiled=True)]
    convert_element_type x1, other arithmetic: 18.4 us -> 21.4 us  [body(): hot = (low == lane & 63).astype(jnp.bfloat16)]
  transfers between devices with their start and end apart: 8 -> 5, of which waited for: 6 -> 5; matrix products, arithmetic and copies ran while one was open for 12% -> 11% of each run, Pallas kernels for 0% -> 0%
where the time goes in v5:
time: 250 us; the launch traced here: 249 us
  waiting for transfers between devices  91.5 us (37%)
  blocking collectives  57.2 us (23%)
  Pallas kernels  37.3 us (15%)
  other arithmetic  25.6 us (10%)
  starting transfers between devices  16.8 us (7%)
  between operations  14.2 us (6%)
  local copies, waits for them, and re-layouts  6.75 us (3%)
    all_gather x1, waiting for transfers between devices, body(): weights = lax.all_gather(coeffs, ('z', 'c'), axis=0, tiled=True)  58 us
    pallas_call x1, Pallas kernels, run_chain(): pl.pallas_call(functools.partial(chain_kernel, 1.0 / math.sqrt(total), se...  35.3 us
    all_to_all x2, blocking collectives, exchange(): return lax.all_to_all(blocks, axis, 0, 0, tiled=True)  33 us
    all_to_all x3, waiting for transfers between devices, exchange(): return lax.all_to_all(blocks, axis, 0, 0, tiled=True)  32.2 us
    all_gather x1, blocking collectives, body(): index = lax.all_gather(pairs, ('z', 'c'), axis=1, tiled=True)  24.2 us
    convert_element_type x1, other arithmetic, body(): hot = (low == lane & 63).astype(jnp.bfloat16)  21.4 us
    all_to_all x3, starting transfers between devices, exchange(): return lax.all_to_all(blocks, axis, 0, 0, tiled=True)  14.8 us
  transfers between devices with their start and end apart: 5, of which 5 were waited for; matrix products, arithmetic and copies ran while one was open for 11% of the time, Pallas kernels for 0%

profile of v5, /device:TPU:8, one launch (start us, length us, event | category | flops | bytes accessed | tf_op | source)
XLA Modules:
  0.0 249.3 jit_solution(11945639944601350635)
XLA Ops:
  7.2 0.0 copy-start.2
  7.2 0.0 all-gather.3.cloned.1.call-start
  7.2 0.7 all-gather.3.cloned.1.call-update
  7.9 24.2 %all-gather = s32[16,2080,2]{1,2,0:T(2,128)S(1)} all-gather(s32[1,2080,2]{1,2,0:T(2,128)} %bitcast.38), channel_id=1, replica_groups=mesh['x'=4,'y'=8,'z'=8,'c'=2] {'z','c'}, dimensions={0}, use_global_device_ids=true | all-gather | bytes 282880 | tf_op jit(solution)/shard_map/all_gather | solution.py:187
  32.1 0.3 reshape.83
  32.4 0.0 copy-done.2
  32.5 0.4 copy.32
  32.9 1.3 constant_dynamic-slice_fusion
  34.2 1.2 slice_reduce_fusion.3
  35.4 21.4 %fusion.hot_hbm = bf16[33280,128]{1,0:T(8,128)(2,1)} fusion(s32[128]{0:T(128)S(1)} %iota_and_fusion, s32[33280]{0:T(1024)S(1)} %get-tuple-element.3, s32[33280]{0:T(1024)S(1)} %get-tuple-element.2, pred[128]{0:T(512)(128)(4,1)S(1)} %iota_compare_fusion.2), kind=kLoop, calls=%fused_computation.1 | loop fusion | flops 17039360 | bytes 8786560 | tf_op jit(solution)/shard_map/convert_element_type | solution.py:192
  56.8 58.0 %all-gather.3.cloned.1.call-done.refs_0_ = bf16[33280,256]{1,0:T(8,128)(2,1)} async-done(((bf16[2080,256]{1,0:T(8,128)(2,1)}), bf16[33280,256]{1,0:T(8,128)(2,1)}) %all-gather.3.cloned.1.call-update) | async-done | bytes 17039376 | tf_op jit(solution)/shard_map/all_gather | solution.py:186
  114.8 35.3 %chain.1 = bf16[8,64,256]{2,1,0:T(8,128)(2,1)} custom-call(f32[8,256]{1,0:T(8,128)} %get-tuple-element.13.state_ref, f32[8,256]{1,0:T(8,128)} %get-tuple-element.12.target_ref, s32[1,33280]{1,0:T(1,128)} %get-tuple-element.9.left_ref, s32[1,33280]{1,0:T(1,128)} %get-tuple-element.8.right_ref, bf16[33280,128]{1,0:T(8,128)(2,1)} %fusion.hot_hbm, ...), custom_call_target="tpu_custom_call" | custom-call | tf_op jit(solution)/shard_map/chain/pallas_call | solution.py:117
  150.1 4.0 %all-to-all-start = ((bf16[8,64,256]{2,1,0:T(8,128)(2,1)}), bf16[8,64,256]{2,1,0:T(8,128)(2,1)S(1)}, u32[]{:S(2)}, u32[]{:S(2)}) async-start(bf16[8,64,256]{2,1,0:T(8,128)(2,1)} %chain.1), calls=%async_computation | async-start | bytes 524288 | tf_op jit(solution)/shard_map/all_to_all | solution.py:169
  154.2 1.2 fusion.1
  155.4 11.1 %all-to-all-done.mine_ref = bf16[8,64,256]{2,1,0:T(8,128)(2,1)S(1)} async-done(((bf16[8,64,256]{2,1,0:T(8,128)(2,1)}), bf16[8,64,256]{2,1,0:T(8,128)(2,1)S(1)}, u32[]{:S(2)}, u32[]{:S(2)}) %all-to-all-start) | async-done | bytes 262176 | tf_op jit(solution)/shard_map/all_to_all | solution.py:169
  166.4 1.9 collective-permute-start
  168.4 0.9 select_bitcast_fusion.1
  169.3 0.6 collective-permute-done.other_ref
  169.9 0.0 copy-start
  169.9 2.0 grad.1
  171.9 0.0 copy-done
  171.9 0.0 copy-start.1
  171.9 19.8 %all_to_all.25 = bf16[4,520,256]{2,1,0:T(8,128)(2,1)S(1)} all-to-all(bf16[4,520,256]{2,1,0:T(8,128)(2,1)S(1)} %bitcast.34), channel_id=1, replica_groups=mesh['x'=4,'y'=8,'z'=8,'c'=2] {'x'}, dimensions={0} | all-to-all | bytes 2129920 | tf_op jit(solution)/shard_map/all_to_all | solution.py:169
  191.7 0.3 reduce_sum.21
  191.9 0.7 pad.14
  192.7 7.3 %all-to-all-start.2 = ((bf16[8,72,256]{2,1,0:T(8,128)(2,1)}), bf16[8,72,256]{2,1,0:T(8,128)(2,1)S(1)}, u32[]{:S(2)}, u32[]{:S(2)}) async-start(bf16[8,72,256]{2,1,0:T(8,128)(2,1)} %bitcast.11), calls=%async_computation.2 | async-start | bytes 589824 | tf_op jit(solution)/shard_map/all_to_all | solution.py:169
  200.0 10.3 %all-to-all-done.2 = bf16[8,72,256]{2,1,0:T(8,128)(2,1)S(1)} async-done(((bf16[8,72,256]{2,1,0:T(8,128)(2,1)}), bf16[8,72,256]{2,1,0:T(8,128)(2,1)S(1)}, u32[]{:S(2)}, u32[]{:S(2)}) %all-to-all-start.2) | async-done | bytes 294944 | tf_op jit(solution)/shard_map/all_to_all | solution.py:169
  210.3 0.0 copy-done.1
  210.3 0.9 multiply_convert_fusion
  211.2 13.3 %all_to_all.26 = bf16[8,72,256]{2,1,0:T(8,128)(2,1)S(1)} all-to-all(bf16[8,72,256]{2,1,0:T(8,128)(2,1)S(1)} %broadcast_in_dim.48), channel_id=1, replica_groups=mesh['x'=4,'y'=8,'z'=8,'c'=2] {'y'}, dimensions={0} | all-to-all | bytes 589824 | tf_op jit(solution)/shard_map/all_to_all | solution.py:169
  224.6 1.0 broadcast_in_dim.49
  225.6 3.5 %all-to-all-start.4 = ((bf16[4,520,256]{2,1,0:T(8,128)(2,1)}), bf16[4,520,256]{2,1,0:T(8,128)(2,1)S(1)}, u32[]{:S(2)}, u32[]{:S(2)}) async-start(bf16[4,520,256]{2,1,0:T(8,128)(2,1)} %broadcast_in_dim.49), calls=%async_computation.4 | async-start | bytes 2129920 | tf_op jit(solution)/shard_map/all_to_all | solution.py:169
  229.1 0.8 fusion.3
  229.9 0.7 copy.29
  230.6 10.9 %all-to-all-done.4 = bf16[4,520,256]{2,1,0:T(8,128)(2,1)S(1)} async-done(((bf16[4,520,256]{2,1,0:T(8,128)(2,1)}), bf16[4,520,256]{2,1,0:T(8,128)(2,1)S(1)}, u32[]{:S(2)}, u32[]{:S(2)}) %all-to-all-start.4) | async-done | bytes 1064992 | tf_op jit(solution)/shard_map/all_to_all | solution.py:169
  241.5 1.0 copy.36
  (10 shorter events, 0.2 us)
Async XLA Ops:
  7.2 25.3 %copy-start.2 = (s32[2,2080]{1,0:T(2,128)S(1)}, s32[2,2080]{1,0:T(2,128)}, u32[]{:S(2)}) copy-start(s32[2,2080]{1,0:T(2,128)} %param.8) | copy-start | bytes 49924
  7.2 107.6 %all-gather.3.cloned.1.call-start = ((), (), s32[]{:S(2)}) async-start(), calls=%async_computation.5 | async-start | bytes 18104320 | tf_op jit(solution)/shard_map/all_gather | solution.py:186
  150.1 16.3 %all-to-all-start = ((bf16[8,64,256]{2,1,0:T(8,128)(2,1)}), bf16[8,64,256]{2,1,0:T(8,128)(2,1)S(1)}, u32[]{:S(2)}, u32[]{:S(2)}) async-start(bf16[8,64,256]{2,1,0:T(8,128)(2,1)} %chain.1), calls=%async_computation | async-start | bytes 524288 | tf_op jit(solution)/shard_map/all_to_all | solution.py:169
  166.4 3.4 %collective-permute-start = (bf16[8,64,256]{2,1,0:T(8,128)(2,1)S(1)}, bf16[8,64,256]{2,1,0:T(8,128)(2,1)S(1)}, u32[]{:S(2)}, u32[]{:S(2)}) collective-permute-start(bf16[8,64,256]{2,1,0:T(8,128)(2,1)S(1)} %all-to-all-done.mine_ref), channel_id=1, source_target_pairs={{0,1},{1,0},{2,3},{3,2},{4,5},{5,4},{6,7},{7,6},{8,9},{9,8},{10,11... | collective-permute-start | bytes 786440 | tf_op jit(solution)/shard_map/ppermute | solution.py:210
  169.9 2.0 copy-start
  171.9 38.4 %copy-start.1 = (bf16[2080,256]{1,0:T(8,128)(2,1)S(1)}, bf16[2080,256]{1,0:T(8,128)(2,1)}, u32[]{:S(2)}) copy-start(bf16[2080,256]{1,0:T(8,128)(2,1)} %param.7) | copy-start | bytes 3194884
  192.7 17.5 %all-to-all-start.2 = ((bf16[8,72,256]{2,1,0:T(8,128)(2,1)}), bf16[8,72,256]{2,1,0:T(8,128)(2,1)S(1)}, u32[]{:S(2)}, u32[]{:S(2)}) async-start(bf16[8,72,256]{2,1,0:T(8,128)(2,1)} %bitcast.11), calls=%async_computation.2 | async-start | bytes 589824 | tf_op jit(solution)/shard_map/all_to_all | solution.py:169
  225.6 15.9 %all-to-all-start.4 = ((bf16[4,520,256]{2,1,0:T(8,128)(2,1)}), bf16[4,520,256]{2,1,0:T(8,128)(2,1)S(1)}, u32[]{:S(2)}, u32[]{:S(2)}) async-start(bf16[4,520,256]{2,1,0:T(8,128)(2,1)} %broadcast_in_dim.49), calls=%async_computation.4 | async-start | bytes 2129920 | tf_op jit(solution)/shard_map/all_to_all | solution.py:169
Sparse Core Ops, SparseCore 0:
  10.1 104.6 all-gather.2

commit v6 on v4

--- a/solution.py
+++ b/solution.py
@@ -12,7 +12,7 @@
 NT = (((1,), (1,)), ((), ()))
 CHUNK = 1664
 FETCH = 2048
-PIECE = 64
+PIECE = 40
 AXES = ("x", "y", "z", "c")
 FULL = pl.BlockSpec(memory_space=pltpu.VMEM)
 
@@ -181,8 +181,6 @@
     core = lax.axis_index("c")
     piece = lax.dynamic_slice_in_dim(coeffs, lax.axis_index("y") * PIECE, PIECE, 0)
     rest = lax.all_gather(coeffs[side:], ("z", "c"), axis=0, tiled=True)
-    mine = spread(spread(piece, "z", nz), "y", ny)
-    other = lax.ppermute(mine, "c", [(0, 1), (1, 0)])
 
     index = spread(pairs[None], ("z", "c"), nz * nc).reshape(nz, nc, 2, -1).transpose(2, 0, 1, 3)
     order = [index[..., side:].reshape(2, -1)]
@@ -190,7 +188,15 @@
     for which in (core, 1 - core):
         part = jnp.where(which == 0, sides[:, :, 0], sides[:, :, 1])
         order.append(part.transpose(0, 2, 1, 3).reshape(2, -1))
-    return [rest, mine, other], jnp.concatenate(order, 1)
+    index = jnp.concatenate(order, 1)
+    lane = jnp.arange(128, dtype=jnp.int32)[None, :]
+    low = jnp.where(lane < 64, index[0][:, None], index[1][:, None]) & 63
+    hot = (low == (lane & 63)).astype(jnp.bfloat16)
+
+    mine = spread(spread(piece, "z", nz), "y", ny)
+    mine, hot = lax.optimization_barrier((mine, hot))
+    other = lax.ppermute(mine, "c", [(0, 1), (1, 0)])
+    return [rest, mine, other], index, hot
 
 
 def body(state, target, coeffs, pairs, mask):
@@ -202,12 +208,9 @@
     core = lax.axis_index("c")
     start = lax.axis_index(("z", "c")) * rows
 
-    blocks, index = gather_candidates(coeffs, pairs)
+    blocks, index, hot = gather_candidates(coeffs, pairs)
     state_own = lax.dynamic_slice_in_dim(state, start, rows, 0)
     target_own = lax.dynamic_slice_in_dim(target, start, rows, 0)
-    lane = jnp.arange(128, dtype=jnp.int32)[None, :]
-    low = jnp.where(lane < 64, index[0][:, None], index[1][:, None]) & 63
-    hot = (low == (lane & 63)).astype(jnp.bfloat16)
     mode = jnp.arange(modes, dtype=jnp.int32)
     left_hot = (pairs[0][:, None] == mode[None, :]).astype(jnp.bfloat16)
     right_hot = (pairs[1][:, None] == mode[None, :]).astype(jnp.bfloat16)

time: 264 us -> 245 us (0.928)
  waiting for transfers between devices: 92 us -> 70.8 us
  starting transfers between devices: 27.1 us -> 30.2 us
  other arithmetic: 22.6 us -> 25.6 us
    all_to_all x5, waiting for transfers between devices: 91.3 us -> 56.7 us  [exchange(): return lax.all_to_all(blocks, axis, 0, 0, tiled=True)]
    all_gather x1, waiting for transfers between devices: 0.02 us -> 12.5 us  [gather_candidates(): rest = lax.all_gather(coeffs[side:], ('z', 'c'), axis=0, tiled=True)]
    convert_element_type x1, other arithmetic: 18.4 us -> 21.4 us  [gather_candidates(): hot = (low == lane & 63).astype(jnp.bfloat16)]
    all_to_all x5, starting transfers between devices: 23 us -> 25.9 us  [exchange(): return lax.all_to_all(blocks, axis, 0, 0, tiled=True)]
  transfers between devices with their start and end apart: 8 -> 8, of which waited for: 6 -> 8; matrix products, arithmetic and copies ran while one was open for 12% -> 13% of each run, Pallas kernels for 0% -> 0%
where the time goes in v6:
time: 245 us; the launch traced here: 244 us
  waiting for transfers between devices  70.8 us (29%)
  blocking collectives  52.9 us (22%)
  Pallas kernels  37.4 us (15%)
  starting transfers between devices  30.2 us (12%)
  other arithmetic  25.6 us (10%)
  between operations  14.3 us (6%)
  local copies, waits for them, and re-layouts  12.4 us (5%)
    all_to_all x5, waiting for transfers between devices, exchange(): return lax.all_to_all(blocks, axis, 0, 0, tiled=True)  56.7 us
    all_to_all x3, blocking collectives, exchange(): return lax.all_to_all(blocks, axis, 0, 0, tiled=True)  52.9 us
    pallas_call x1, Pallas kernels, run_chain(): pl.pallas_call(functools.partial(chain_kernel, 1.0 / math.sqrt(total), se...  35.3 us
    all_to_all x5, starting transfers between devices, exchange(): return lax.all_to_all(blocks, axis, 0, 0, tiled=True)  25.9 us
    convert_element_type x1, other arithmetic, gather_candidates(): hot = (low == lane & 63).astype(jnp.bfloat16)  21.4 us
    all_gather x1, waiting for transfers between devices, gather_candidates(): rest = lax.all_gather(coeffs[side:], ('z', 'c'), axis=0, tiled=True)  12.5 us
  transfers between devices with their start and end apart: 8, of which 8 were waited for; matrix products, arithmetic and copies ran while one was open for 13% of the time, Pallas kernels for 0%

profile of v6, /device:TPU:8, one launch (start us, length us, event | category | flops | bytes accessed | tf_op | source)
XLA Modules:
  0.0 243.6 jit_solution(15276727585115972660)
XLA Ops:
  7.2 0.0 copy-start.3
  7.2 0.0 all-gather.2.cloned.1.call-start
  7.2 2.2 slice.54
  9.4 0.0 all-gather.2.cloned.1.call-update
  9.4 0.7 constant_dynamic-slice_fusion
  10.2 19.9 %all_to_all.40 = bf16[8,40,256]{2,1,0:T(8,128)(2,1)S(1)} all-to-all(bf16[8,40,256]{2,1,0:T(8,128)(2,1)S(1)} %broadcast_in_dim.62), channel_id=1, replica_groups=mesh['x'=4,'y'=8,'z'=8,'c'=2] {'z'}, dimensions={0} | all-to-all | bytes 327680 | tf_op jit(solution)/shard_map/all_to_all | solution.py:170
  30.0 0.0 copy-done.3
  30.0 0.8 broadcast_in_dim.61
  30.8 3.5 %all-to-all-start = ((s32[16,1,2,2080]{3,2,1,0:T(2,128)}), s32[16,1,2,2080]{3,2,1,0:T(2,128)S(1)}, u32[]{:S(2)}, u32[]{:S(2)}) async-start(s32[16,1,2,2080]{3,2,1,0:T(2,128)} %broadcast_in_dim.61), calls=%async_computation | async-start | bytes 557056 | tf_op jit(solution)/shard_map/all_to_all | solution.py:170
  34.4 14.7 %all-to-all-done = s32[16,1,2,2080]{3,2,1,0:T(2,128)S(1)} async-done(((s32[16,1,2,2080]{3,2,1,0:T(2,128)}), s32[16,1,2,2080]{3,2,1,0:T(2,128)S(1)}, u32[]{:S(2)}, u32[]{:S(2)}) %all-to-all-start) | async-done | bytes 266272 | tf_op jit(solution)/shard_map/all_to_all | solution.py:170
  49.1 1.2 broadcast_in_dim.64
  50.3 7.5 %all-to-all-start.2 = ((bf16[8,320,256]{2,1,0:T(8,128)(2,1)}), bf16[8,320,256]{2,1,0:T(8,128)(2,1)S(1)}, u32[]{:S(2)}, u32[]{:S(2)}) async-start(bf16[8,320,256]{2,1,0:T(8,128)(2,1)} %broadcast_in_dim.64), calls=%async_computation.2 | async-start | bytes 2621440 | tf_op jit(solution)/shard_map/all_to_all | solution.py:170
  57.8 0.3 slice.62
  58.1 0.1 copy.44
  58.3 0.4 reshape.100
  58.7 0.1 reshape.101
  58.8 0.1 reshape.102
  59.0 0.1 reshape.103
  59.1 1.2 slice_reduce_fusion.3
  60.3 21.4 %fusion.hot_hbm = bf16[33280,128]{1,0:T(8,128)(2,1)} fusion(s32[128]{0:T(128)S(1)} %iota_and_fusion, s32[33280]{0:T(1024)S(1)} %get-tuple-element.7, s32[33280]{0:T(1024)S(1)} %get-tuple-element.6, pred[128]{0:T(512)(128)(4,1)S(1)} %iota_compare_fusion.2), kind=kLoop, calls=%fused_computation.1 | loop fusion | flops 17039360 | bytes 8786560 | tf_op jit(solution)/shard_map/convert_element_type | solution.py:194
  81.7 9.8 %all-to-all-done.2 = bf16[8,320,256]{2,1,0:T(8,128)(2,1)S(1)} async-done(((bf16[8,320,256]{2,1,0:T(8,128)(2,1)}), bf16[8,320,256]{2,1,0:T(8,128)(2,1)S(1)}, u32[]{:S(2)}, u32[]{:S(2)}) %all-to-all-start.2) | async-done | bytes 1310752 | tf_op jit(solution)/shard_map/all_to_all | solution.py:170
  91.5 0.0 copy-start.1
  91.5 2.1 collective-permute-start
  93.6 0.4 copy.51
  94.0 1.3 constant_dynamic-slice_fusion.1
  95.3 1.2 collective-permute-done.refs_2_
  96.5 12.5 %all-gather.2.cloned.1.call-done.refs_0_ = bf16[28160,256]{1,0:T(8,128)(2,1)} async-done(((bf16[1760,256]{1,0:T(8,128)(2,1)}), bf16[28160,256]{1,0:T(8,128)(2,1)}) %all-gather.2.cloned.1.call-update) | async-done | bytes 14417936 | tf_op jit(solution)/shard_map/all_gather | solution.py:183
  109.0 0.0 copy-done.1
  109.0 35.3 %chain.1 = bf16[8,64,256]{2,1,0:T(8,128)(2,1)} custom-call(f32[8,256]{1,0:T(8,128)} %get-tuple-element.19.state_ref, f32[8,256]{1,0:T(8,128)} %get-tuple-element.18.target_ref, s32[1,33280]{1,0:T(1,128)} %get-tuple-element.13.left_ref, s32[1,33280]{1,0:T(1,128)} %get-tuple-element.12.right_ref, bf16[33280,128]{1,0:T(8,128)(2,1)} %fusion.hot_hbm, ...), custom_call_target="tpu_custom_call" | custom-call | tf_op jit(solution)/shard_map/chain/pallas_call | solution.py:118
  144.4 4.0 %all-to-all-start.3 = ((bf16[8,64,256]{2,1,0:T(8,128)(2,1)}), bf16[8,64,256]{2,1,0:T(8,128)(2,1)S(1)}, u32[]{:S(2)}, u32[]{:S(2)}) async-start(bf16[8,64,256]{2,1,0:T(8,128)(2,1)} %chain.1), calls=%async_computation.3 | async-start | bytes 524288 | tf_op jit(solution)/shard_map/all_to_all | solution.py:170
  148.4 1.2 fusion.1
  149.6 11.1 %all-to-all-done.3.mine_ref = bf16[8,64,256]{2,1,0:T(8,128)(2,1)S(1)} async-done(((bf16[8,64,256]{2,1,0:T(8,128)(2,1)}), bf16[8,64,256]{2,1,0:T(8,128)(2,1)S(1)}, u32[]{:S(2)}, u32[]{:S(2)}) %all-to-all-start.3) | async-done | bytes 262176 | tf_op jit(solution)/shard_map/all_to_all | solution.py:170
  160.7 2.1 collective-permute-start.1
  162.8 0.9 select_bitcast_fusion.1
  163.7 0.4 collective-permute-done.1.other_ref
  164.1 0.0 copy-start
  164.1 2.1 grad.1
  166.2 0.0 copy-done
  166.2 0.0 copy-start.2
  166.2 19.8 %all_to_all.41 = bf16[4,520,256]{2,1,0:T(8,128)(2,1)S(1)} all-to-all(bf16[4,520,256]{2,1,0:T(8,128)(2,1)S(1)} %bitcast.49), channel_id=1, replica_groups=mesh['x'=4,'y'=8,'z'=8,'c'=2] {'x'}, dimensions={0} | all-to-all | bytes 2129920 | tf_op jit(solution)/shard_map/all_to_all | solution.py:170
  186.0 0.3 reduce_sum.21
  186.2 0.7 pad.14
  187.0 7.3 %all-to-all-start.5 = ((bf16[8,72,256]{2,1,0:T(8,128)(2,1)}), bf16[8,72,256]{2,1,0:T(8,128)(2,1)S(1)}, u32[]{:S(2)}, u32[]{:S(2)}) async-start(bf16[8,72,256]{2,1,0:T(8,128)(2,1)} %bitcast.17), calls=%async_computation.5 | async-start | bytes 589824 | tf_op jit(solution)/shard_map/all_to_all | solution.py:170
  194.2 10.3 %all-to-all-done.5 = bf16[8,72,256]{2,1,0:T(8,128)(2,1)S(1)} async-done(((bf16[8,72,256]{2,1,0:T(8,128)(2,1)}), bf16[8,72,256]{2,1,0:T(8,128)(2,1)S(1)}, u32[]{:S(2)}, u32[]{:S(2)}) %all-to-all-start.5) | async-done | bytes 294944 | tf_op jit(solution)/shard_map/all_to_all | solution.py:170
  204.5 0.0 copy-done.2
  204.5 0.9 multiply_convert_fusion
  205.5 13.3 %all_to_all.42 = bf16[8,72,256]{2,1,0:T(8,128)(2,1)S(1)} all-to-all(bf16[8,72,256]{2,1,0:T(8,128)(2,1)S(1)} %broadcast_in_dim.70), channel_id=1, replica_groups=mesh['x'=4,'y'=8,'z'=8,'c'=2] {'y'}, dimensions={0} | all-to-all | bytes 589824 | tf_op jit(solution)/shard_map/all_to_all | solution.py:170
  218.8 1.0 broadcast_in_dim.71
  219.9 3.5 %all-to-all-start.7 = ((bf16[4,520,256]{2,1,0:T(8,128)(2,1)}), bf16[4,520,256]{2,1,0:T(8,128)(2,1)S(1)}, u32[]{:S(2)}, u32[]{:S(2)}) async-start(bf16[4,520,256]{2,1,0:T(8,128)(2,1)} %broadcast_in_dim.71), calls=%async_computation.7 | async-start | bytes 2129920 | tf_op jit(solution)/shard_map/all_to_all | solution.py:170
  223.4 0.8 fusion.3
  224.2 0.7 copy.48
  224.9 10.9 %all-to-all-done.7 = bf16[4,520,256]{2,1,0:T(8,128)(2,1)S(1)} async-done(((bf16[4,520,256]{2,1,0:T(8,128)(2,1)}), bf16[4,520,256]{2,1,0:T(8,128)(2,1)S(1)}, u32[]{:S(2)}, u32[]{:S(2)}) %all-to-all-start.7) | async-done | bytes 1064992 | tf_op jit(solution)/shard_map/all_to_all | solution.py:170
  235.7 1.0 copy.57
  (18 shorter events, 0.3 us)
Async XLA Ops:
  7.2 22.9 %copy-start.3 = (s32[2,2080]{1,0:T(2,128)S(1)}, s32[2,2080]{1,0:T(2,128)}, u32[]{:S(2)}) copy-start(s32[2,2080]{1,0:T(2,128)} %param.8) | copy-start | bytes 49924
  7.2 101.8 %all-gather.2.cloned.1.call-start = ((), (), s32[]{:S(2)}) async-start(), calls=%async_computation.8 | async-start | bytes 15319040 | tf_op jit(solution)/shard_map/all_gather | solution.py:183
  30.8 18.3 %all-to-all-start = ((s32[16,1,2,2080]{3,2,1,0:T(2,128)}), s32[16,1,2,2080]{3,2,1,0:T(2,128)S(1)}, u32[]{:S(2)}, u32[]{:S(2)}) async-start(s32[16,1,2,2080]{3,2,1,0:T(2,128)} %broadcast_in_dim.61), calls=%async_computation | async-start | bytes 557056 | tf_op jit(solution)/shard_map/all_to_all | solution.py:170
  50.3 41.2 %all-to-all-start.2 = ((bf16[8,320,256]{2,1,0:T(8,128)(2,1)}), bf16[8,320,256]{2,1,0:T(8,128)(2,1)S(1)}, u32[]{:S(2)}, u32[]{:S(2)}) async-start(bf16[8,320,256]{2,1,0:T(8,128)(2,1)} %broadcast_in_dim.64), calls=%async_computation.2 | async-start | bytes 2621440 | tf_op jit(solution)/shard_map/all_to_all | solution.py:170
  91.5 17.6 %copy-start.1 = (bf16[8,320,256]{2,1,0:T(8,128)(2,1)}, bf16[8,320,256]{2,1,0:T(8,128)(2,1)S(1)}, u32[]{:S(2)}) copy-start(bf16[8,320,256]{2,1,0:T(8,128)(2,1)S(1)} %all-to-all-done.2) | copy-start | bytes 3932164
  91.5 5.0 %collective-permute-start = (bf16[2560,256]{1,0:T(8,128)(2,1)S(1)}, bf16[2560,256]{1,0:T(8,128)(2,1)}, u32[]{:S(2)}, u32[]{:S(2)}) collective-permute-start(bf16[2560,256]{1,0:T(8,128)(2,1)S(1)} %bitcast.50), channel_id=1, source_target_pairs={{0,1},{1,0},{2,3},{3,2},{4,5},{5,4},{6,7},{7,6},{8,9},{9,8},{10,11... | collective-permute-start | bytes 3932168 | tf_op jit(solution)/shard_map/ppermute | solution.py:198
  144.4 16.3 %all-to-all-start.3 = ((bf16[8,64,256]{2,1,0:T(8,128)(2,1)}), bf16[8,64,256]{2,1,0:T(8,128)(2,1)S(1)}, u32[]{:S(2)}, u32[]{:S(2)}) async-start(bf16[8,64,256]{2,1,0:T(8,128)(2,1)} %chain.1), calls=%async_computation.3 | async-start | bytes 524288 | tf_op jit(solution)/shard_map/all_to_all | solution.py:170
  160.7 3.4 %collective-permute-start.1 = (bf16[8,64,256]{2,1,0:T(8,128)(2,1)S(1)}, bf16[8,64,256]{2,1,0:T(8,128)(2,1)S(1)}, u32[]{:S(2)}, u32[]{:S(2)}) collective-permute-start(bf16[8,64,256]{2,1,0:T(8,128)(2,1)S(1)} %all-to-all-done.3.mine_ref), channel_id=1, source_target_pairs={{0,1},{1,0},{2,3},{3,2},{4,5},{5,4},{6,7},{7,6},{8,9},{9,8},{10,11... | collective-permute-start | bytes 786440 | tf_op jit(solution)/shard_map/ppermute | solution.py:231
  164.1 2.1 copy-start
  166.2 38.3 %copy-start.2 = (bf16[2080,256]{1,0:T(8,128)(2,1)S(1)}, bf16[2080,256]{1,0:T(8,128)(2,1)}, u32[]{:S(2)}) copy-start(bf16[2080,256]{1,0:T(8,128)(2,1)} %param.7) | copy-start | bytes 3194884
  187.0 17.5 %all-to-all-start.5 = ((bf16[8,72,256]{2,1,0:T(8,128)(2,1)}), bf16[8,72,256]{2,1,0:T(8,128)(2,1)S(1)}, u32[]{:S(2)}, u32[]{:S(2)}) async-start(bf16[8,72,256]{2,1,0:T(8,128)(2,1)} %bitcast.17), calls=%async_computation.5 | async-start | bytes 589824 | tf_op jit(solution)/shard_map/all_to_all | solution.py:170
  219.9 15.9 %all-to-all-start.7 = ((bf16[4,520,256]{2,1,0:T(8,128)(2,1)}), bf16[4,520,256]{2,1,0:T(8,128)(2,1)S(1)}, u32[]{:S(2)}, u32[]{:S(2)}) async-start(bf16[4,520,256]{2,1,0:T(8,128)(2,1)} %broadcast_in_dim.71), calls=%async_computation.7 | async-start | bytes 2129920 | tf_op jit(solution)/shard_map/all_to_all | solution.py:170
Sparse Core Ops, SparseCore 0:
  10.7 98.2 all-gather.1

commit v7 on v6

--- a/solution.py
+++ b/solution.py
@@ -12,7 +12,7 @@
 NT = (((1,), (1,)), ((), ()))
 CHUNK = 1664
 FETCH = 2048
-PIECE = 40
+PIECE = 48
 AXES = ("x", "y", "z", "c")
 FULL = pl.BlockSpec(memory_space=pltpu.VMEM)
 

time: 245 us -> 242 us (0.988)
  waiting for transfers between devices: 70.8 us -> 67.8 us
    all_gather x1, waiting for transfers between devices: 12.5 us -> 2.89 us  [gather_candidates(): rest = lax.all_gather(coeffs[side:], ('z', 'c'), axis=0, tiled=True)]
    all_to_all x5, waiting for transfers between devices: 56.7 us -> 62.7 us  [exchange(): return lax.all_to_all(blocks, axis, 0, 0, tiled=True)]
where the time goes in v7:
time: 242 us; the launch traced here: 241 us
  waiting for transfers between devices  67.8 us (28%)
  blocking collectives  53.7 us (22%)
  Pallas kernels  37.4 us (15%)
  starting transfers between devices  30.2 us (12%)
  other arithmetic  25.6 us (11%)
  between operations  14.3 us (6%)
  local copies, waits for them, and re-layouts  12.3 us (5%)
    all_to_all x5, waiting for transfers between devices, exchange(): return lax.all_to_all(blocks, axis, 0, 0, tiled=True)  62.7 us
    all_to_all x3, blocking collectives, exchange(): return lax.all_to_all(blocks, axis, 0, 0, tiled=True)  53.7 us
    pallas_call x1, Pallas kernels, run_chain(): pl.pallas_call(functools.partial(chain_kernel, 1.0 / math.sqrt(total), se...  35.3 us
    all_to_all x5, starting transfers between devices, exchange(): return lax.all_to_all(blocks, axis, 0, 0, tiled=True)  25.9 us
    convert_element_type x1, other arithmetic, gather_candidates(): hot = (low == lane & 63).astype(jnp.bfloat16)  21.4 us
  transfers between devices with their start and end apart: 8, of which 8 were waited for; matrix products, arithmetic and copies ran while one was open for 13% of the time, Pallas kernels for 0%

profile of v7, /device:TPU:8, one launch (start us, length us, event | category | flops | bytes accessed | tf_op | source)
XLA Modules:
  0.0 241.1 jit_solution(9877319524374329967)
XLA Ops:
  7.2 0.0 copy-start.3
  7.2 0.0 all-gather.2.cloned.1.call-start
  7.2 2.1 slice.54
  9.3 0.0 all-gather.2.cloned.1.call-update
  9.4 0.7 constant_dynamic-slice_fusion
  10.1 20.6 %all_to_all.40 = bf16[8,48,256]{2,1,0:T(8,128)(2,1)S(1)} all-to-all(bf16[8,48,256]{2,1,0:T(8,128)(2,1)S(1)} %broadcast_in_dim.62), channel_id=1, replica_groups=mesh['x'=4,'y'=8,'z'=8,'c'=2] {'z'}, dimensions={0} | all-to-all | bytes 393216 | tf_op jit(solution)/shard_map/all_to_all | solution.py:170
  30.7 0.0 copy-done.3
  30.7 0.8 broadcast_in_dim.61
  31.5 3.5 %all-to-all-start = ((s32[16,1,2,2080]{3,2,1,0:T(2,128)}), s32[16,1,2,2080]{3,2,1,0:T(2,128)S(1)}, u32[]{:S(2)}, u32[]{:S(2)}) async-start(s32[16,1,2,2080]{3,2,1,0:T(2,128)} %broadcast_in_dim.61), calls=%async_computation | async-start | bytes 557056 | tf_op jit(solution)/shard_map/all_to_all | solution.py:170
  35.1 14.7 %all-to-all-done = s32[16,1,2,2080]{3,2,1,0:T(2,128)S(1)} async-done(((s32[16,1,2,2080]{3,2,1,0:T(2,128)}), s32[16,1,2,2080]{3,2,1,0:T(2,128)S(1)}, u32[]{:S(2)}, u32[]{:S(2)}) %all-to-all-start) | async-done | bytes 266272 | tf_op jit(solution)/shard_map/all_to_all | solution.py:170
  49.8 1.3 broadcast_in_dim.64
  51.1 7.6 %all-to-all-start.2 = ((bf16[8,384,256]{2,1,0:T(8,128)(2,1)}), bf16[8,384,256]{2,1,0:T(8,128)(2,1)S(1)}, u32[]{:S(2)}, u32[]{:S(2)}) async-start(bf16[8,384,256]{2,1,0:T(8,128)(2,1)} %broadcast_in_dim.64), calls=%async_computation.2 | async-start | bytes 3145728 | tf_op jit(solution)/shard_map/all_to_all | solution.py:170
  58.7 0.1 copy.44
  58.8 0.4 reshape.100
  59.2 0.1 reshape.101
  59.4 0.1 reshape.102
  59.5 0.1 reshape.103
  59.7 1.2 slice_reduce_fusion.3
  60.9 21.4 %fusion.hot_hbm = bf16[33280,128]{1,0:T(8,128)(2,1)} fusion(s32[128]{0:T(128)S(1)} %iota_and_fusion, s32[33280]{0:T(1024)S(1)} %get-tuple-element.7, s32[33280]{0:T(1024)S(1)} %get-tuple-element.6, pred[128]{0:T(512)(128)(4,1)S(1)} %iota_compare_fusion.2), kind=kLoop, calls=%fused_computation.1 | loop fusion | flops 17039360 | bytes 8786560 | tf_op jit(solution)/shard_map/convert_element_type | solution.py:194
  82.3 15.7 %all-to-all-done.2 = bf16[8,384,256]{2,1,0:T(8,128)(2,1)S(1)} async-done(((bf16[8,384,256]{2,1,0:T(8,128)(2,1)}), bf16[8,384,256]{2,1,0:T(8,128)(2,1)S(1)}, u32[]{:S(2)}, u32[]{:S(2)}) %all-to-all-start.2) | async-done | bytes 1572896 | tf_op jit(solution)/shard_map/all_to_all | solution.py:170
  97.9 0.0 copy-start.1
  97.9 2.1 collective-permute-start
  100.0 0.4 copy.51
  100.4 1.3 constant_dynamic-slice_fusion.1
  101.8 1.9 collective-permute-done.refs_2_
  103.7 2.9 %all-gather.2.cloned.1.call-done.refs_0_ = bf16[27136,256]{1,0:T(8,128)(2,1)} async-done(((bf16[1696,256]{1,0:T(8,128)(2,1)}), bf16[27136,256]{1,0:T(8,128)(2,1)}) %all-gather.2.cloned.1.call-update) | async-done | bytes 13893648 | tf_op jit(solution)/shard_map/all_gather | solution.py:183
  106.5 0.0 copy-done.1
  106.5 35.3 %chain.1 = bf16[8,64,256]{2,1,0:T(8,128)(2,1)} custom-call(f32[8,256]{1,0:T(8,128)} %get-tuple-element.19.state_ref, f32[8,256]{1,0:T(8,128)} %get-tuple-element.18.target_ref, s32[1,33280]{1,0:T(1,128)} %get-tuple-element.13.left_ref, s32[1,33280]{1,0:T(1,128)} %get-tuple-element.12.right_ref, bf16[33280,128]{1,0:T(8,128)(2,1)} %fusion.hot_hbm, ...), custom_call_target="tpu_custom_call" | custom-call | tf_op jit(solution)/shard_map/chain/pallas_call | solution.py:118
  141.9 4.1 %all-to-all-start.3 = ((bf16[8,64,256]{2,1,0:T(8,128)(2,1)}), bf16[8,64,256]{2,1,0:T(8,128)(2,1)S(1)}, u32[]{:S(2)}, u32[]{:S(2)}) async-start(bf16[8,64,256]{2,1,0:T(8,128)(2,1)} %chain.1), calls=%async_computation.3 | async-start | bytes 524288 | tf_op jit(solution)/shard_map/all_to_all | solution.py:170
  145.9 1.2 fusion.1
  147.1 11.1 %all-to-all-done.3.mine_ref = bf16[8,64,256]{2,1,0:T(8,128)(2,1)S(1)} async-done(((bf16[8,64,256]{2,1,0:T(8,128)(2,1)}), bf16[8,64,256]{2,1,0:T(8,128)(2,1)S(1)}, u32[]{:S(2)}, u32[]{:S(2)}) %all-to-all-start.3) | async-done | bytes 262176 | tf_op jit(solution)/shard_map/all_to_all | solution.py:170
  158.2 2.1 collective-permute-start.1
  160.4 0.9 select_bitcast_fusion.1
  161.3 0.4 collective-permute-done.1.other_ref
  161.6 0.0 copy-start
  161.6 2.0 grad.1
  163.7 0.0 copy-done
  163.7 0.0 copy-start.2
  163.7 19.8 %all_to_all.41 = bf16[4,520,256]{2,1,0:T(8,128)(2,1)S(1)} all-to-all(bf16[4,520,256]{2,1,0:T(8,128)(2,1)S(1)} %bitcast.49), channel_id=1, replica_groups=mesh['x'=4,'y'=8,'z'=8,'c'=2] {'x'}, dimensions={0} | all-to-all | bytes 2129920 | tf_op jit(solution)/shard_map/all_to_all | solution.py:170
  183.5 0.3 reduce_sum.21
  183.7 0.7 pad.14
  184.5 7.3 %all-to-all-start.5 = ((bf16[8,72,256]{2,1,0:T(8,128)(2,1)}), bf16[8,72,256]{2,1,0:T(8,128)(2,1)S(1)}, u32[]{:S(2)}, u32[]{:S(2)}) async-start(bf16[8,72,256]{2,1,0:T(8,128)(2,1)} %bitcast.17), calls=%async_computation.5 | async-start | bytes 589824 | tf_op jit(solution)/shard_map/all_to_all | solution.py:170
  191.7 10.3 %all-to-all-done.5 = bf16[8,72,256]{2,1,0:T(8,128)(2,1)S(1)} async-done(((bf16[8,72,256]{2,1,0:T(8,128)(2,1)}), bf16[8,72,256]{2,1,0:T(8,128)(2,1)S(1)}, u32[]{:S(2)}, u32[]{:S(2)}) %all-to-all-start.5) | async-done | bytes 294944 | tf_op jit(solution)/shard_map/all_to_all | solution.py:170
  202.1 0.0 copy-done.2
  202.1 0.9 multiply_convert_fusion
  203.0 13.3 %all_to_all.42 = bf16[8,72,256]{2,1,0:T(8,128)(2,1)S(1)} all-to-all(bf16[8,72,256]{2,1,0:T(8,128)(2,1)S(1)} %broadcast_in_dim.70), channel_id=1, replica_groups=mesh['x'=4,'y'=8,'z'=8,'c'=2] {'y'}, dimensions={0} | all-to-all | bytes 589824 | tf_op jit(solution)/shard_map/all_to_all | solution.py:170
  216.4 1.0 broadcast_in_dim.71
  217.4 3.5 %all-to-all-start.7 = ((bf16[4,520,256]{2,1,0:T(8,128)(2,1)}), bf16[4,520,256]{2,1,0:T(8,128)(2,1)S(1)}, u32[]{:S(2)}, u32[]{:S(2)}) async-start(bf16[4,520,256]{2,1,0:T(8,128)(2,1)} %broadcast_in_dim.71), calls=%async_computation.7 | async-start | bytes 2129920 | tf_op jit(solution)/shard_map/all_to_all | solution.py:170
  220.9 0.8 fusion.3
  221.7 0.7 copy.48
  222.4 10.9 %all-to-all-done.7 = bf16[4,520,256]{2,1,0:T(8,128)(2,1)S(1)} async-done(((bf16[4,520,256]{2,1,0:T(8,128)(2,1)}), bf16[4,520,256]{2,1,0:T(8,128)(2,1)S(1)}, u32[]{:S(2)}, u32[]{:S(2)}) %all-to-all-start.7) | async-done | bytes 1064992 | tf_op jit(solution)/shard_map/all_to_all | solution.py:170
  233.3 1.0 copy.57
  (19 shorter events, 0.3 us)
Async XLA Ops:
  7.2 23.6 %copy-start.3 = (s32[2,2080]{1,0:T(2,128)S(1)}, s32[2,2080]{1,0:T(2,128)}, u32[]{:S(2)}) copy-start(s32[2,2080]{1,0:T(2,128)} %param.8) | copy-start | bytes 49924
  7.2 99.4 %all-gather.2.cloned.1.call-start = ((), (), s32[]{:S(2)}) async-start(), calls=%async_computation.8 | async-start | bytes 14761984 | tf_op jit(solution)/shard_map/all_gather | solution.py:183
  31.5 18.3 %all-to-all-start = ((s32[16,1,2,2080]{3,2,1,0:T(2,128)}), s32[16,1,2,2080]{3,2,1,0:T(2,128)S(1)}, u32[]{:S(2)}, u32[]{:S(2)}) async-start(s32[16,1,2,2080]{3,2,1,0:T(2,128)} %broadcast_in_dim.61), calls=%async_computation | async-start | bytes 557056 | tf_op jit(solution)/shard_map/all_to_all | solution.py:170
  51.1 46.8 %all-to-all-start.2 = ((bf16[8,384,256]{2,1,0:T(8,128)(2,1)}), bf16[8,384,256]{2,1,0:T(8,128)(2,1)S(1)}, u32[]{:S(2)}, u32[]{:S(2)}) async-start(bf16[8,384,256]{2,1,0:T(8,128)(2,1)} %broadcast_in_dim.64), calls=%async_computation.2 | async-start | bytes 3145728 | tf_op jit(solution)/shard_map/all_to_all | solution.py:170
  97.9 8.6 %copy-start.1 = (bf16[8,384,256]{2,1,0:T(8,128)(2,1)}, bf16[8,384,256]{2,1,0:T(8,128)(2,1)S(1)}, u32[]{:S(2)}) copy-start(bf16[8,384,256]{2,1,0:T(8,128)(2,1)S(1)} %all-to-all-done.2) | copy-start | bytes 4718596
  97.9 5.7 %collective-permute-start = (bf16[3072,256]{1,0:T(8,128)(2,1)S(1)}, bf16[3072,256]{1,0:T(8,128)(2,1)}, u32[]{:S(2)}, u32[]{:S(2)}) collective-permute-start(bf16[3072,256]{1,0:T(8,128)(2,1)S(1)} %bitcast.50), channel_id=1, source_target_pairs={{0,1},{1,0},{2,3},{3,2},{4,5},{5,4},{6,7},{7,6},{8,9},{9,8},{10,11... | collective-permute-start | bytes 4718600 | tf_op jit(solution)/shard_map/ppermute | solution.py:198
  141.9 16.3 %all-to-all-start.3 = ((bf16[8,64,256]{2,1,0:T(8,128)(2,1)}), bf16[8,64,256]{2,1,0:T(8,128)(2,1)S(1)}, u32[]{:S(2)}, u32[]{:S(2)}) async-start(bf16[8,64,256]{2,1,0:T(8,128)(2,1)} %chain.1), calls=%async_computation.3 | async-start | bytes 524288 | tf_op jit(solution)/shard_map/all_to_all | solution.py:170
  158.2 3.4 %collective-permute-start.1 = (bf16[8,64,256]{2,1,0:T(8,128)(2,1)S(1)}, bf16[8,64,256]{2,1,0:T(8,128)(2,1)S(1)}, u32[]{:S(2)}, u32[]{:S(2)}) collective-permute-start(bf16[8,64,256]{2,1,0:T(8,128)(2,1)S(1)} %all-to-all-done.3.mine_ref), channel_id=1, source_target_pairs={{0,1},{1,0},{2,3},{3,2},{4,5},{5,4},{6,7},{7,6},{8,9},{9,8},{10,11... | collective-permute-start | bytes 786440 | tf_op jit(solution)/shard_map/ppermute | solution.py:231
  161.6 2.0 copy-start
  163.7 38.4 %copy-start.2 = (bf16[2080,256]{1,0:T(8,128)(2,1)S(1)}, bf16[2080,256]{1,0:T(8,128)(2,1)}, u32[]{:S(2)}) copy-start(bf16[2080,256]{1,0:T(8,128)(2,1)} %param.7) | copy-start | bytes 3194884
  184.5 17.6 %all-to-all-start.5 = ((bf16[8,72,256]{2,1,0:T(8,128)(2,1)}), bf16[8,72,256]{2,1,0:T(8,128)(2,1)S(1)}, u32[]{:S(2)}, u32[]{:S(2)}) async-start(bf16[8,72,256]{2,1,0:T(8,128)(2,1)} %bitcast.17), calls=%async_computation.5 | async-start | bytes 589824 | tf_op jit(solution)/shard_map/all_to_all | solution.py:170
  217.4 15.9 %all-to-all-start.7 = ((bf16[4,520,256]{2,1,0:T(8,128)(2,1)}), bf16[4,520,256]{2,1,0:T(8,128)(2,1)S(1)}, u32[]{:S(2)}, u32[]{:S(2)}) async-start(bf16[4,520,256]{2,1,0:T(8,128)(2,1)} %broadcast_in_dim.71), calls=%async_computation.7 | async-start | bytes 2129920 | tf_op jit(solution)/shard_map/all_to_all | solution.py:170
Sparse Core Ops, SparseCore 0:
  10.7 95.7 all-gather.1
